TPU v7x, 256 devices: a whole 4x4x8 slice. The times are simulated.
256 devices in a mesh: rec: 16 (over y_lo, z), lig: 8 (over y_hi, x), slab: 2 (over core).
Axes of the slice: x: 4, y: 4 (y_hi: 2, y_lo: 2; y = y_hi * 2 + y_lo), z: 8, core: 2. Of those that a mesh axis runs over, the one named last changes fastest.
Arguments:
- receptors: float32 [16, 4, 64, 4096], P('rec', None, 'slab'), may hold values from -6 to 6
- ligands: float32 [128, 4, 64, 4096], P(('rec', 'lig'), None, 'slab'), may hold values from -6 to 6
- plan: int32 [1], replicated, may hold values from 0 to 15
- rotations: int32 [2], replicated, may hold values from 0 to 7
Outputs:
- scores: float32 [1, 2, 128, 64, 4096], P(None, None, ('rec', 'lig'), 'slab')
All inputs are finite; a program needn't handle non-finite values.
Results may differ from a plain program's by a relative error of at most 0.0003.
Values sent between devices are 32-bit elements; how exact they have to be, the bound alone decides.
No kernel may reach another device: no remote copies, remote signals or barrier semaphores. Data moves between devices by JAX's collectives and lax.ppermute only.
A program may use at most 192 MiB of HBM per device.

v0:
```python
import math

import jax
import jax.numpy as jnp
import ml_dtypes
import numpy as np
from jax import lax
from jax.experimental import pallas as pl
from jax.experimental.pallas import tpu as pltpu
from jax.sharding import PartitionSpec as P

F32 = jnp.float32
BF16 = jnp.bfloat16


def split_table(table):
    high = table.astype(ml_dtypes.bfloat16)
    low = (table - high.astype(np.float64)).astype(ml_dtypes.bfloat16)
    return high, low


ROTATIONS = [
    (False, 1, 1, 1),
    (True, -1, 1, 1),
    (False, -1, 1, -1),
    (True, 1, 1, -1),
    (False, -1, -1, 1),
    (True, 1, -1, 1),
    (False, 1, -1, -1),
    (True, -1, -1, -1),
]


def dft(n):
    phase = np.outer(np.arange(n), np.arange(n)) % n * (2 * math.pi / n)
    return np.cos(phase), np.sin(phase)


def lane_table(n, swap, sy, sz):
    cos, sin = dft(n)
    eye = np.eye(2)
    real = np.concatenate([np.kron(eye, cos), np.kron(eye, -sz * sin)], axis=1)
    imag = np.concatenate([np.kron(eye, sy * sz * sin), np.kron(eye, sy * cos)], axis=1)
    table = np.concatenate([real, imag], axis=0)
    if swap:
        rows = table.reshape(2, 2, n, 4 * n)
        table = rows.transpose(1, 0, 2, 3).reshape(4 * n, 4 * n)
    return table


def row_table(n, sx):
    cos, sin = dft(n)
    return np.concatenate(
        [np.concatenate([cos, sx * sin], axis=1), np.concatenate([-sx * sin, cos], axis=1)], axis=0
    )


def lane_stack(table):
    high, low = split_table(table)
    return np.concatenate([high, high, low], axis=0)


def row_stack(table):
    high, low = split_table(table)
    return np.concatenate([high, low, high], axis=1)


def split(value):
    high = value.astype(BF16)
    return high, (value - high.astype(F32)).astype(BF16)


def lane_dot(value, table):
    high, low = split(value)
    return jnp.dot(
        jnp.concatenate([high, low, high], axis=1), table, preferred_element_type=F32
    )


def row_dot(table, value):
    high, low = split(value)
    return jnp.dot(
        table, jnp.concatenate([high, high, low], axis=0), preferred_element_type=F32
    )


def times_phase(value, cos, sin):
    re, im = value
    if im is None:
        return re * cos, -(re * sin)
    if abs(cos - sin) < 1e-12:
        return (re + im) * cos, (im - re) * cos
    return re * cos + im * sin, im * cos - re * sin


def real_forward(values):
    size = len(values)
    if size == 2:
        return [(values[0] + values[1], None), (values[0] - values[1], None)]
    even, odd = real_forward(values[0::2]), real_forward(values[1::2])
    out = [None] * (size // 2 + 1)
    out[0] = (even[0][0] + odd[0][0], None)
    out[size // 2] = (even[0][0] - odd[0][0], None)
    for k in range(1, size // 4):
        angle = 2 * math.pi * k / size
        re, im = times_phase(odd[k], math.cos(angle), math.sin(angle))
        out[k] = (even[k][0] + re, even[k][1] + im)
        out[size // 2 - k] = (even[k][0] - re, im - even[k][1])
    out[size // 4] = (even[size // 4][0], -odd[size // 4][0])
    return out


def real_inverse(spectrum):
    size = 2 * (len(spectrum) - 1)
    if size == 2:
        first, second = spectrum[0][0], spectrum[1][0]
        return [first + second, first - second]
    half, quarter = size // 2, size // 4
    even, odd = [None] * (quarter + 1), [None] * (quarter + 1)
    even[0] = (spectrum[0][0] + spectrum[half][0], None)
    odd[0] = (spectrum[0][0] - spectrum[half][0], None)
    for k in range(1, quarter):
        (ar, ai), (br, bi) = spectrum[k], spectrum[half - k]
        even[k] = (ar + br, ai - bi)
        angle = 2 * math.pi * k / size
        cos, sin = math.cos(angle), math.sin(angle)
        dr, di = ar - br, ai + bi
        if abs(cos - sin) < 1e-12:
            odd[k] = ((dr - di) * cos, (di + dr) * cos)
        else:
            odd[k] = (dr * cos - di * sin, di * cos + dr * sin)
    re, im = spectrum[quarter]
    even[quarter] = (re + re, None)
    odd[quarter] = (-(im + im), None)
    evens, odds = real_inverse(even), real_inverse(odd)
    return [value for pair in zip(evens, odds) for value in pair]


def lane_consts(width):
    left = lax.broadcasted_iota(jnp.int32, (8, width), 1) < width // 2
    one, zero = jnp.ones((8, width), F32), jnp.zeros((8, width), F32)
    return left, one, zero


def y_forward(load, count):
    width = 128
    left, one, zero = lane_consts(width)
    sign = jnp.where(left, one, -one)
    spectrum = real_forward([load(b) for b in range(count)])
    units = []
    first = spectrum[0][0]
    middle = spectrum[count // 2][0]
    units.append((first * sign + pltpu.roll(first, width // 2, 1), middle * sign))
    for k in range(1, count // 2):
        angle = 2 * math.pi * k / (2 * count)
        cos = jnp.where(left, one, math.cos(angle) * one)
        sin = jnp.where(left, zero, math.sin(angle) * one)
        re, im = spectrum[k]
        turned_re = re * cos + im * sin
        turned_im = im * cos - re * sin
        units.append(
            (
                turned_re * sign + pltpu.roll(turned_re, width // 2, 1),
                turned_im + pltpu.roll(turned_im, width // 2, 1) * sign,
            )
        )
    return units


def y_inverse(units):
    width = 128
    count = 2 * len(units)
    left, one, zero = lane_consts(width)
    sign = jnp.where(left, one, -one)
    spectrum = [None] * (count // 2 + 1)
    first, middle = units[0]
    spectrum[0] = (first * sign + pltpu.roll(first, width // 2, 1), None)
    spectrum[count // 2] = (middle * (sign + sign), None)
    for k in range(1, count // 2):
        angle = 2 * math.pi * k / (2 * count)
        cos = jnp.where(left, one, math.cos(angle) * one)
        sin = jnp.where(left, zero, math.sin(angle) * one)
        re, im = units[k]
        sum_re = re * sign + pltpu.roll(re, width // 2, 1)
        sum_im = im - pltpu.roll(im, width // 2, 1) * sign
        spectrum[k] = (sum_re * cos - sum_im * sin, sum_im * cos + sum_re * sin)
    return real_inverse(spectrum)


def forward_y_kernel(place_ref, grid_ref, mine_ref, other_ref):
    rows, width = grid_ref.shape
    count = width // 128

    def run(low_ref, high_ref):
        def step(tile, carry):
            at = pl.ds(pl.multiple_of(tile * 8, 8), 8)
            units = y_forward(lambda b: grid_ref[at, b * 128 : (b + 1) * 128], count)
            half = len(units) // 2
            for k, (re, im) in enumerate(units):
                out = low_ref if k < half else high_ref
                out[2 * (k % half), at, :] = re
                out[2 * (k % half) + 1, at, :] = im
            return carry

        lax.fori_loop(0, rows // 8, step, 0)

    @pl.when(place_ref[0] == 0)
    def _():
        run(mine_ref, other_ref)

    @pl.when(place_ref[0] == 1)
    def _():
        run(other_ref, mine_ref)


def forward_y(place, grid, block, steps, first):
    width = grid.shape[1]
    pieces = width // 256
    out = jax.ShapeDtypeStruct((pieces, block * steps, 128), F32)
    spec = pl.BlockSpec((pieces, block, 128), lambda i, place: (0, i, 0))
    return pl.pallas_call(
        forward_y_kernel,
        grid_spec=pltpu.PrefetchScalarGridSpec(
            num_scalar_prefetch=1,
            grid=(steps,),
            in_specs=[pl.BlockSpec((block, width), lambda i, place: (first(place) + i, 0))],
            out_specs=[spec, spec],
        ),
        out_shape=[out, out],
    )(place, grid)


def unit_tiles(step, place, first_re, first_im):
    odd = (place == 1).astype(F32)
    left = lax.broadcasted_iota(jnp.int32, first_re.shape, 1) < first_re.shape[1] // 2
    mask = jnp.where(left, 1.0 - odd, 0.0)
    rolled = pltpu.roll(first_im, first_im.shape[1] // 2, 1)
    keep = jnp.where(step == 1, odd, 1.0)
    extra = step == 0
    re = jnp.where(extra, first_im * mask, first_re)
    im = jnp.where(extra, rolled * mask, first_im * keep)
    return re, im


def spectrum_kernel(place_ref, turn_ref, mine_ref, other_ref, lane_ref, row_ref, out_ref, work):
    step = pl.program_id(1)
    slot = pl.program_id(0)
    place = place_ref[0]
    length = 64
    channels = mine_ref.shape[1] // 32
    swapped = lax.rem(turn_ref[slot], 2) == 1

    def tiles(c):
        at = pl.ds(c * 32, 32)
        own_re, own_im = mine_ref[0, at, :], mine_ref[1, at, :]
        far_re, far_im = other_ref[0, at, :], other_ref[1, at, :]
        is_low = place == 0
        re = jnp.concatenate(
            [jnp.where(is_low, own_re, far_re), jnp.where(is_low, far_re, own_re)], axis=0
        )
        im = jnp.concatenate(
            [jnp.where(is_low, own_im, far_im), jnp.where(is_low, far_im, own_im)], axis=0
        )
        return unit_tiles(step, place, re, im)

    @pl.when(jnp.logical_not(swapped))
    def _():
        for c in range(channels):
            re, im = tiles(c)
            work[c * 64 : (c + 1) * 64, :128] = re
            work[c * 64 : (c + 1) * 64, 128:] = im

    @pl.when(swapped)
    def _():
        for c in range(channels):
            re, im = tiles(c)
            turned = jnp.concatenate([re, im], axis=0).T
            work[c * 64 : (c + 1) * 64, :128] = turned[:length]
            work[c * 64 : (c + 1) * 64, 128:] = turned[length:]

    along = lane_dot(work[...], lane_ref[0])
    for c in range(channels):
        part = along[c * 64 : (c + 1) * 64]
        both = jnp.concatenate([part[:, :128], part[:, 128:]], axis=0)
        out_ref[0, 0, c] = row_dot(row_ref[0], both)


def spectrum(place, turns, mine, other, lane_tables, row_tables):
    pieces, rows, _ = mine.shape
    steps = pieces // 2 + 1
    slots = turns.shape[0]
    channels = rows // 32
    unit = pl.BlockSpec((2, rows, 128), lambda i, u, place, turns: (jnp.maximum(u - 1, 0), 0, 0))
    return pl.pallas_call(
        spectrum_kernel,
        grid_spec=pltpu.PrefetchScalarGridSpec(
            num_scalar_prefetch=2,
            grid=(slots, steps),
            in_specs=[
                unit,
                unit,
                pl.BlockSpec((1, 768, 256), lambda i, u, place, turns: (turns[i], 0, 0)),
                pl.BlockSpec((1, 128, 384), lambda i, u, place, turns: (turns[i], 0, 0)),
            ],
            out_specs=pl.BlockSpec(
                (1, 1, channels, 128, 128), lambda i, u, place, turns: (i, u, 0, 0, 0)
            ),
            scratch_shapes=[pltpu.VMEM((rows * 2, 256), F32)],
        ),
        out_shape=jax.ShapeDtypeStruct((slots, steps, channels, 128, 128), F32),
    )(place, turns, mine, other, lane_tables, row_tables)


def product_kernel(
    place_ref, rec_ref, lig_ref, lane_ref, row_ref, back_lane_ref, back_row_ref,
    mine_ref, other_ref, extra, planes,
):
    step = pl.program_id(0)
    place = place_ref[0]
    channels = lig_ref.shape[2]
    slots = lig_ref.shape[0]
    per = rec_ref.shape[0] // channels
    grids = []
    for c in range(channels):
        parts = [
            [rec_ref[c * per + p, part, s] for s in range(2) for p in range(per)] for part in range(2)
        ]
        re, im = (jnp.concatenate(piece, axis=0) for piece in parts)
        re, im = unit_tiles(step, place, re, im)
        grids.append(jnp.concatenate([re, im], axis=1))
    along = lane_dot(jnp.concatenate(grids, axis=0), lane_ref[...])
    sums = [None] * slots
    for c in range(channels):
        part = along[c * 64 : (c + 1) * 64]
        both = jnp.concatenate([part[:, :128], part[:, 128:]], axis=0)
        rec = row_dot(row_ref[...], both)
        rec_re, rec_im = rec[:64], rec[64:]
        for i in range(slots):
            re, im = lig_ref[i, 0, c, :64], lig_ref[i, 0, c, 64:]
            term = (rec_re * re + rec_im * im, rec_re * im - rec_im * re)
            sums[i] = term if c == 0 else (sums[i][0] + term[0], sums[i][1] + term[1])
    both = jnp.concatenate([jnp.concatenate(s, axis=0) for s in sums], axis=1)
    rows = row_dot(back_row_ref[...], both)
    lanes = jnp.concatenate(
        [
            jnp.concatenate([rows[:64, i * 128 : (i + 1) * 128], rows[64:, i * 128 : (i + 1) * 128]], axis=1)
            for i in range(slots)
        ],
        axis=0,
    )
    back = lane_dot(lanes, back_lane_ref[...])
    re, im = back[:, :128], back[:, 128:]

    @pl.when(step == 0)
    def _():
        left = lax.broadcasted_iota(jnp.int32, re.shape, 1) < 64
        extra[...] = jnp.where(left, re, pltpu.roll(im, 64, 1))

    @pl.when(step > 0)
    def _():
        first = jnp.logical_and(step == 1, place == 0)
        planes[0] = re.reshape(slots, 64, 128)
        planes[1] = jnp.where(first, extra[...], im).reshape(slots, 64, 128)
        own = pl.ds(pl.multiple_of(place * 32, 32), 32)
        far = pl.ds(pl.multiple_of(32 - place * 32, 32), 32)
        for part in range(2):
            for i in range(slots):
                mine_ref[part, i] = planes[part, i, own, :]
                other_ref[part, i] = planes[part, i, far, :]


def product(place, rec, lig, tables):
    slots, steps, channels = lig.shape[:3]
    pieces = rec.shape[1]
    out = jax.ShapeDtypeStruct((pieces, slots, 32, 128), F32)
    unit = lambda u, place: (jnp.maximum(u - 1, 0), 0, 0, 0)
    whole = lambda t: pl.BlockSpec(t.shape, lambda u, place: (0, 0))
    return pl.pallas_call(
        product_kernel,
        grid_spec=pltpu.PrefetchScalarGridSpec(
            num_scalar_prefetch=1,
            grid=(steps,),
            in_specs=[
                pl.BlockSpec(
                    (rec.shape[0], 2, 2, rec.shape[3], 128),
                    lambda u, place: (0, jnp.maximum(u - 1, 0), 0, 0, 0),
                ),
                pl.BlockSpec((slots, 1, channels, 128, 128), lambda u, place: (0, u, 0, 0, 0)),
                *[whole(t) for t in tables],
            ],
            out_specs=[pl.BlockSpec((2, slots, 32, 128), unit)] * 2,
            scratch_shapes=[
                pltpu.VMEM((slots * 64, 128), F32),
                pltpu.VMEM((2, slots, 64, 128), F32),
            ],
        ),
        out_shape=[out, out],
    )(place, rec, lig, *tables)


def inverse_y_kernel(place_ref, mine_ref, other_ref, out_ref):
    pieces, slots, rows, _ = mine_ref.shape
    is_low = place_ref[0] == 0

    def step(tile, carry):
        slot = tile // (rows // 8)
        at = pl.ds(pl.multiple_of(tile % (rows // 8) * 8, 8), 8)
        low, high = [], []
        for k in range(pieces // 2):
            own = [mine_ref[2 * k + part, slot, at, :] for part in range(2)]
            far = [other_ref[2 * k + part, slot, at, :] for part in range(2)]
            low.append(tuple(jnp.where(is_low, a, b) for a, b in zip(own, far)))
            high.append(tuple(jnp.where(is_low, b, a) for a, b in zip(own, far)))
        for b, value in enumerate(y_inverse(low + high)):
            out_ref[slot, at, b * 128 : (b + 1) * 128] = value
        return carry

    lax.fori_loop(0, slots * (rows // 8), step, 0)


def inverse_y(place, mine, other):
    pieces, slots, rows, _ = mine.shape
    return pl.pallas_call(
        inverse_y_kernel,
        grid_spec=pltpu.PrefetchScalarGridSpec(
            num_scalar_prefetch=1,
            grid=(1,),
            in_specs=[pl.BlockSpec(mine.shape, lambda i, place: (0, 0, 0, 0))] * 2,
            out_specs=pl.BlockSpec((slots, rows, pieces * 256), lambda i, place: (0, 0, 0)),
        ),
        out_shape=jax.ShapeDtypeStruct((slots, rows, pieces * 256), F32),
    )(place, mine, other)


def per_device(receptors, ligands, plan, rotations):
    _, channels, half, flat = ligands.shape
    length = 2 * half
    core = lax.axis_index("slab")
    lig_index = lax.axis_index("lig")
    place = jnp.stack([core, lig_index]).astype(jnp.int32)
    swap = lambda value: lax.ppermute(value, "slab", [(0, 1), (1, 0)])
    lane_tables = jnp.asarray(
        np.stack([lane_stack(lane_table(length, swapped, sy, sz)) for swapped, _, sy, sz in ROTATIONS])
    )
    row_tables = jnp.asarray(np.stack([row_stack(row_table(length, sx)) for _, sx, _, _ in ROTATIONS]))
    factor = 1.0 / (math.sqrt(channels * length**3) * length**3)
    tables = [
        jnp.asarray(lane_stack(lane_table(length, False, 1, 1))),
        jnp.asarray(row_stack(row_table(length, 1))),
        jnp.asarray(lane_stack(lane_table(length, False, 1, -1) * factor)),
        jnp.asarray(row_stack(row_table(length, -1))),
    ]

    rec_rows = receptors.reshape(channels * half, flat)
    share = channels * half // lax.axis_size("lig")
    rec_mine, rec_other = forward_y(place, rec_rows, share, 1, lambda place: place[1])
    rec_far = swap(rec_other)
    is_low = core == 0
    rec_share = jnp.stack(
        [jnp.where(is_low, rec_mine, rec_far), jnp.where(is_low, rec_far, rec_mine)], axis=1
    )
    scattered = lax.all_to_all(rec_share, "rec", split_axis=0, concat_axis=0)
    piece = lax.dynamic_index_in_dim(scattered, plan[0], 0, True)
    gathered = lax.all_to_all(
        jnp.broadcast_to(piece, rec_share.shape), "rec", split_axis=0, concat_axis=0
    )
    spread = lax.all_to_all(
        jnp.broadcast_to(gathered[None], (lax.axis_size("lig"), *gathered.shape)),
        "lig",
        split_axis=0,
        concat_axis=0,
    )

    lig_rows = ligands.reshape(channels * half, flat)
    lig_mine, lig_other = forward_y(place, lig_rows, half, channels, lambda place: 0)
    lig_far = swap(lig_other)
    lig_spec = spectrum(place, rotations, lig_mine, lig_far, lane_tables, row_tables)

    out_mine, out_other = product(place, spread, lig_spec, tables)
    out_far = swap(out_other)
    scores = inverse_y(place, out_mine, out_far)
    return scores[None, :, None]


def solution(mesh):
    return jax.shard_map(
        per_device,
        mesh=mesh,
        in_specs=(P("rec", None, "slab", None), P(("rec", "lig"), None, "slab", None), P(), P()),
        out_specs=P(None, None, ("rec", "lig"), "slab", None),
        check_vma=False,
    )
```

profile of v0, /device:TPU:1, one launch (start us, length us, event | category | flops | bytes accessed | tf_op | source)
XLA Modules:
  0.0 100.4 jit_solution(10838084210415529248)
XLA Ops:
  0.0 0.6 pad_add_fusion.place_ref
  0.6 2.6 %shard_map.100 = (f32[16,16,128]{2,1,0:T(8,128)}, f32[16,16,128]{2,1,0:T(8,128)}) custom-call(s32[2]{0:T(128)} %pad_add_fusion.place_ref, f32[128,4096]{1,0:T(8,128)} %bitcast.17), custom_call_target="tpu_custom_call" | custom-call | tf_op jit(solution)/shard_map/pallas_call | solution.py:221
  3.2 3.2 %collective-permute-start = (f32[16,16,128]{2,1,0:T(8,128)}, f32[16,16,128]{2,1,0:T(8,128)S(1)}, u32[]{:S(2)}, u32[]{:S(2)}) collective-permute-start(f32[16,16,128]{2,1,0:T(8,128)} %get-tuple-element.12), channel_id=1, source_target_pairs={{0,1},{1,0},{2,3},{3,2},{4,5},{5,4},{6,7},{7,6},{8,9},{9,8},{10,11... | collective-permute-start | bytes 393224 | tf_op jit(solution)/shard_map/ppermute | solution.py:441
  6.4 1.2 %collective-permute-done = f32[16,16,128]{2,1,0:T(8,128)S(1)} collective-permute-done((f32[16,16,128]{2,1,0:T(8,128)}, f32[16,16,128]{2,1,0:T(8,128)S(1)}, u32[]{:S(2)}, u32[]{:S(2)}) %collective-permute-start) | collective-permute-done | bytes 131104 | tf_op jit(solution)/shard_map/ppermute | solution.py:441
  7.6 0.9 select_bitcast_fusion.1
  8.6 0.7 copy.12
  9.3 7.6 %all-to-all-start = ((f32[16,2,16,128]{3,2,1,0:T(8,128)}), f32[16,2,16,128]{3,2,1,0:T(8,128)S(1)}, u32[]{:S(2)}, u32[]{:S(2)}) async-start(f32[16,2,16,128]{3,2,1,0:T(8,128)} %copy.12), calls=%async_computation | async-start | bytes 524288 | tf_op jit(solution)/shard_map/all_to_all | solution.py:462
  17.5 8.3 %all-to-all-done = f32[16,2,16,128]{3,2,1,0:T(8,128)S(1)} async-done(((f32[16,2,16,128]{3,2,1,0:T(8,128)}), f32[16,2,16,128]{3,2,1,0:T(8,128)S(1)}, u32[]{:S(2)}, u32[]{:S(2)}) %all-to-all-start) | async-done | bytes 262176 | tf_op jit(solution)/shard_map/all_to_all | solution.py:462
  25.9 13.1 %all_to_all.15 = f32[16,2,16,128]{3,2,1,0:T(8,128)S(1)} all-to-all(f32[16,2,16,128]{3,2,1,0:T(8,128)S(1)} %broadcast_in_dim.17), channel_id=1, replica_groups=mesh['rec'=16,'lig'=8,'slab'=2] {'rec'}, dimensions={0} | all-to-all | bytes 524288 | tf_op jit(solution)/shard_map/all_to_all | solution.py:464
  38.9 1.6 %broadcast_in_dim.18 = f32[8,16,2,16,128]{4,3,2,1,0:T(8,128)} broadcast(f32[16,2,16,128]{3,2,1,0:T(8,128)S(1)} %all_to_all.15), dimensions={1,2,3,4} | broadcast | bytes 2359296 | tf_op jit(solution)/shard_map/broadcast_in_dim | solution.py:468
  40.6 6.4 %all-to-all-start.2 = ((f32[8,16,2,16,128]{4,3,2,1,0:T(8,128)}), f32[8,16,2,16,128]{4,3,2,1,0:T(8,128)S(1)}, u32[]{:S(2)}, u32[]{:S(2)}) async-start(f32[8,16,2,16,128]{4,3,2,1,0:T(8,128)} %broadcast_in_dim.18), calls=%async_computation.2 | async-start | bytes 4194304 | tf_op jit(solution)/shard_map/all_to_all | solution.py:467
  46.9 5.5 %shard_map.101 = (f32[16,128,128]{2,1,0:T(8,128)}, f32[16,128,128]{2,1,0:T(8,128)}) custom-call(s32[2]{0:T(128)} %pad_add_fusion.place_ref, f32[128,4096]{1,0:T(8,128)} %bitcast.18), custom_call_target="tpu_custom_call" | custom-call | tf_op jit(solution)/shard_map/pallas_call | solution.py:221
  52.4 3.5 %collective-permute-start.1 = (f32[16,128,128]{2,1,0:T(8,128)}, f32[16,128,128]{2,1,0:T(8,128)S(1)}, u32[]{:S(2)}, u32[]{:S(2)}) collective-permute-start(f32[16,128,128]{2,1,0:T(8,128)} %get-tuple-element.14), channel_id=1, source_target_pairs={{0,1},{1,0},{2,3},{3,2},{4,5},{5,4},{6,7},{7,6},{8,9},{9,8},{10,11... | collective-permute-start | bytes 3145736 | tf_op jit(solution)/shard_map/ppermute | solution.py:441
  55.9 2.5 %collective-permute-done.1.other_ref = f32[16,128,128]{2,1,0:T(8,128)S(1)} collective-permute-done((f32[16,128,128]{2,1,0:T(8,128)}, f32[16,128,128]{2,1,0:T(8,128)S(1)}, u32[]{:S(2)}, u32[]{:S(2)}) %collective-permute-start.1) | collective-permute-done | bytes 1048608 | tf_op jit(solution)/shard_map/ppermute | solution.py:441
  58.4 0.0 copy-start.1
  58.4 1.0 copy-done.1
  59.4 19.5 %shard_map.102.lig_ref = f32[2,9,4,128,128]{4,3,2,1,0:T(8,128)} custom-call(s32[2]{0:T(128)} %pad_add_fusion.place_ref, s32[2]{0:T(128)} %turn_ref.1, f32[16,128,128]{2,1,0:T(8,128)} %get-tuple-element.13.mine_ref, f32[16,128,128]{2,1,0:T(8,128)} %copy-done.1, bf16[8,768,256]{2,1,0:T(8,128)(2,1)} %constant.27.clone.lane_ref, ...), custom_call_target="tpu_custom_call" | custom-call | tf_op jit(solution)/shard_map/pallas_call | solution.py:294
  78.8 0.0 all-to-all-done.2.rec_ref
  78.9 1.4 %copy-done = f32[8,16,2,16,128]{4,3,2,1,0:T(8,128)} copy-done((f32[8,16,2,16,128]{4,3,2,1,0:T(8,128)}, f32[8,16,2,16,128]{4,3,2,1,0:T(8,128)S(1)}, u32[]{:S(2)}) %copy-start) | copy-done | bytes 2097176
  80.2 13.3 %shard_map.103 = (f32[16,2,32,128]{3,2,1,0:T(8,128)}, f32[16,2,32,128]{3,2,1,0:T(8,128)}) custom-call(s32[2]{0:T(128)} %pad_add_fusion.place_ref, f32[8,16,2,16,128]{4,3,2,1,0:T(8,128)} %copy-done, f32[2,9,4,128,128]{4,3,2,1,0:T(8,128)} %shard_map.102.lig_ref, bf16[768,256]{1,0:T(8,128)(2,1)} %constant.29.clone.lane_ref, ...), custom_call_target="tpu_custom_call" | custom-call | tf_op jit(solution)/shard_map/pallas_call | solution.py:378
  93.5 0.4 collective-permute-start.2
  93.9 1.7 %collective-permute-done.2.other_ref = f32[16,2,32,128]{3,2,1,0:T(8,128)S(1)} collective-permute-done((f32[16,2,32,128]{3,2,1,0:T(8,128)}, f32[16,2,32,128]{3,2,1,0:T(8,128)S(1)}, u32[]{:S(2)}, u32[]{:S(2)}) %collective-permute-start.2) | collective-permute-done | bytes 524320 | tf_op jit(solution)/shard_map/ppermute | solution.py:441
  95.6 0.8 copy-done.2
  96.4 3.9 %shard_map.104 = f32[2,32,4096]{2,1,0:T(8,128)} custom-call(s32[2]{0:T(128)} %pad_add_fusion.place_ref, f32[16,2,32,128]{3,2,1,0:T(8,128)} %get-tuple-element.15.mine_ref, f32[16,2,32,128]{3,2,1,0:T(8,128)} %copy-done.2), custom_call_target="tpu_custom_call" | custom-call | tf_op jit(solution)/shard_map/pallas_call | solution.py:423
  (5 shorter events, 0.0 us)
Async XLA Ops:
  3.2 4.4 %collective-permute-start = (f32[16,16,128]{2,1,0:T(8,128)}, f32[16,16,128]{2,1,0:T(8,128)S(1)}, u32[]{:S(2)}, u32[]{:S(2)}) collective-permute-start(f32[16,16,128]{2,1,0:T(8,128)} %get-tuple-element.12), channel_id=1, source_target_pairs={{0,1},{1,0},{2,3},{3,2},{4,5},{5,4},{6,7},{7,6},{8,9},{9,8},{10,11... | collective-permute-start | bytes 393224 | tf_op jit(solution)/shard_map/ppermute | solution.py:441
  9.3 16.5 %all-to-all-start = ((f32[16,2,16,128]{3,2,1,0:T(8,128)}), f32[16,2,16,128]{3,2,1,0:T(8,128)S(1)}, u32[]{:S(2)}, u32[]{:S(2)}) async-start(f32[16,2,16,128]{3,2,1,0:T(8,128)} %copy.12), calls=%async_computation | async-start | bytes 524288 | tf_op jit(solution)/shard_map/all_to_all | solution.py:462
  40.6 38.3 %all-to-all-start.2 = ((f32[8,16,2,16,128]{4,3,2,1,0:T(8,128)}), f32[8,16,2,16,128]{4,3,2,1,0:T(8,128)S(1)}, u32[]{:S(2)}, u32[]{:S(2)}) async-start(f32[8,16,2,16,128]{4,3,2,1,0:T(8,128)} %broadcast_in_dim.18), calls=%async_computation.2 | async-start | bytes 4194304 | tf_op jit(solution)/shard_map/all_to_all | solution.py:467
  52.4 6.0 %collective-permute-start.1 = (f32[16,128,128]{2,1,0:T(8,128)}, f32[16,128,128]{2,1,0:T(8,128)S(1)}, u32[]{:S(2)}, u32[]{:S(2)}) collective-permute-start(f32[16,128,128]{2,1,0:T(8,128)} %get-tuple-element.14), channel_id=1, source_target_pairs={{0,1},{1,0},{2,3},{3,2},{4,5},{5,4},{6,7},{7,6},{8,9},{9,8},{10,11... | collective-permute-start | bytes 3145736 | tf_op jit(solution)/shard_map/ppermute | solution.py:441
  58.4 1.0 copy-start.1
  78.9 1.4 %copy-start = (f32[8,16,2,16,128]{4,3,2,1,0:T(8,128)}, f32[8,16,2,16,128]{4,3,2,1,0:T(8,128)S(1)}, u32[]{:S(2)}) copy-start(f32[8,16,2,16,128]{4,3,2,1,0:T(8,128)S(1)} %all-to-all-done.2.rec_ref) | copy-start | bytes 6291460
  93.5 2.1 %collective-permute-start.2 = (f32[16,2,32,128]{3,2,1,0:T(8,128)}, f32[16,2,32,128]{3,2,1,0:T(8,128)S(1)}, u32[]{:S(2)}, u32[]{:S(2)}) collective-permute-start(f32[16,2,32,128]{3,2,1,0:T(8,128)} %get-tuple-element.16), channel_id=1, source_target_pairs={{0,1},{1,0},{2,3},{3,2},{4,5},{5,4},{6,7},{7,6},{8,9},{9,8},{10,11... | collective-permute-start | bytes 1572872 | tf_op jit(solution)/shard_map/ppermute | solution.py:441
  95.6 0.8 copy-start.2
where the time goes:
time: 102 us; the launch traced here: 100 us
  Pallas kernels  44.7 us (44%)
  starting transfers between devices  21.1 us (21%)
  waiting for transfers between devices  13.7 us (13%)
  blocking collectives  13.1 us (13%)
  local copies, waits for them, and re-layouts  5.54 us (5%)
  other arithmetic  1.53 us (2%)
    pallas_call x1, Pallas kernels, spectrum(): pl.pallas_call(spectrum_kernel, grid_spec=pltpu.PrefetchScalarGridSpec(nu...  19.5 us
    pallas_call x1, Pallas kernels, product(): pl.pallas_call(product_kernel, grid_spec=pltpu.PrefetchScalarGridSpec(num...  13.3 us
    all_to_all x1, blocking collectives, per_device(): lax.all_to_all(jnp.broadcast_to(piece, rec_share.shape), 'rec', split_axi...  13.1 us
    all_to_all x1, waiting for transfers between devices, per_device(): scattered = lax.all_to_all(rec_share, 'rec', split_axis=0, concat_axis=0)  8.3 us
    pallas_call x2, Pallas kernels, forward_y(): pl.pallas_call(forward_y_kernel, grid_spec=pltpu.PrefetchScalarGridSpec(n...  8.04 us
    all_to_all x1, starting transfers between devices, per_device(): scattered = lax.all_to_all(rec_share, 'rec', split_axis=0, concat_axis=0)  7.57 us
    ppermute x3, starting transfers between devices, per_device(): swap = lambda value: lax.ppermute(value, 'slab', [(0, 1), (1, 0)])  7.14 us
    all_to_all x1, starting transfers between devices, per_device(): lax.all_to_all(jnp.broadcast_to(gathered[None], (lax.axis_size('lig'), *g...  6.36 us
  transfers between devices with their start and end apart: 5, of which 4 were waited for; matrix products, arithmetic and copies ran while one was open for 0% of the time, Pallas kernels for 25%

commit v1 on v0

v1 whole, which is shorter than its diff:
```python
import math

import jax
import jax.numpy as jnp
import numpy as np
from jax import lax
from jax.experimental import pallas as pl
from jax.experimental.pallas import tpu as pltpu
from jax.sharding import Mesh, PartitionSpec as P

F32 = jnp.float32
BF16 = jnp.bfloat16
VMEM = pl.BlockSpec(memory_space=pltpu.VMEM)
SMEM = pl.BlockSpec(memory_space=pltpu.SMEM)
UNROLL = 4
COLORS = 4


ROTATIONS = [
    (False, 1, 1, 1),
    (True, -1, 1, 1),
    (False, -1, 1, -1),
    (True, 1, 1, -1),
    (False, -1, -1, 1),
    (True, 1, -1, 1),
    (False, 1, -1, -1),
    (True, -1, -1, -1),
]


def dft(n):
    phase = np.outer(np.arange(n), np.arange(n)) % n * (2 * math.pi / n)
    return np.cos(phase), np.sin(phase)


def base_tables(n):
    cos, sin = dft(n)
    eye = np.eye(2)
    plain = np.block([[np.kron(eye, cos), np.kron(eye, -sin)], [np.kron(eye, sin), np.kron(eye, cos)]])
    turned = plain.reshape(2, 2, n, 4 * n).transpose(1, 0, 2, 3).reshape(4 * n, 4 * n)
    rows = np.block([[cos, sin], [-sin, cos]])
    return np.stack([plain, turned]).astype(np.float32), rows.astype(np.float32)


SIGNS = np.array([[signs[1], signs[2], signs[3]] for signs in ROTATIONS], np.float32)


def split(value):
    high = value.astype(BF16)
    return high, (value - high.astype(F32)).astype(BF16)


def lane_stack(table):
    high, low = split(table)
    return jnp.concatenate([high, high, low], axis=0)


def row_stack(table):
    high, low = split(table)
    return jnp.concatenate([high, low, high], axis=1)


def lane_dot(value, table):
    high, low = split(value)
    return jnp.dot(jnp.concatenate([high, low, high], axis=1), table, preferred_element_type=F32)


def row_dot(table, value):
    high, low = split(value)
    return jnp.dot(table, jnp.concatenate([high, high, low], axis=0), preferred_element_type=F32)


def times_phase(value, cos, sin):
    re, im = value
    if im is None:
        return re * cos, -(re * sin)
    if abs(cos - sin) < 1e-12:
        return (re + im) * cos, (im - re) * cos
    return re * cos + im * sin, im * cos - re * sin


def real_forward(values):
    size = len(values)
    if size == 2:
        return [(values[0] + values[1], None), (values[0] - values[1], None)]
    even, odd = real_forward(values[0::2]), real_forward(values[1::2])
    out = [None] * (size // 2 + 1)
    out[0] = (even[0][0] + odd[0][0], None)
    out[size // 2] = (even[0][0] - odd[0][0], None)
    for k in range(1, size // 4):
        angle = 2 * math.pi * k / size
        re, im = times_phase(odd[k], math.cos(angle), math.sin(angle))
        out[k] = (even[k][0] + re, even[k][1] + im)
        out[size // 2 - k] = (even[k][0] - re, im - even[k][1])
    out[size // 4] = (even[size // 4][0], -odd[size // 4][0])
    return out


def real_inverse(spectrum):
    size = 2 * (len(spectrum) - 1)
    if size == 2:
        first, second = spectrum[0][0], spectrum[1][0]
        return [first + second, first - second]
    half, quarter = size // 2, size // 4
    even, odd = [None] * (quarter + 1), [None] * (quarter + 1)
    even[0] = (spectrum[0][0] + spectrum[half][0], None)
    odd[0] = (spectrum[0][0] - spectrum[half][0], None)
    for k in range(1, quarter):
        (ar, ai), (br, bi) = spectrum[k], spectrum[half - k]
        even[k] = (ar + br, ai - bi)
        angle = 2 * math.pi * k / size
        cos, sin = math.cos(angle), math.sin(angle)
        dr, di = ar - br, ai + bi
        if abs(cos - sin) < 1e-12:
            odd[k] = ((dr - di) * cos, (di + dr) * cos)
        else:
            odd[k] = (dr * cos - di * sin, di * cos + dr * sin)
    re, im = spectrum[quarter]
    even[quarter] = (re + re, None)
    odd[quarter] = (-(im + im), None)
    evens, odds = real_inverse(even), real_inverse(odd)
    return [value for pair in zip(evens, odds) for value in pair]


def lane_consts(width):
    left = lax.broadcasted_iota(jnp.int32, (8, width), 1) < width // 2
    one, zero = jnp.ones((8, width), F32), jnp.zeros((8, width), F32)
    return left, one, zero


def y_forward(load, count):
    width = 128
    left, one, zero = lane_consts(width)
    sign = jnp.where(left, one, -one)
    spectrum = real_forward([load(b) for b in range(count)])
    units = []
    first = spectrum[0][0]
    middle = spectrum[count // 2][0]
    units.append((first * sign + pltpu.roll(first, width // 2, 1), middle * sign))
    for k in range(1, count // 2):
        angle = 2 * math.pi * k / (2 * count)
        cos = jnp.where(left, one, math.cos(angle) * one)
        sin = jnp.where(left, zero, math.sin(angle) * one)
        re, im = spectrum[k]
        turned_re = re * cos + im * sin
        turned_im = im * cos - re * sin
        units.append(
            (
                turned_re * sign + pltpu.roll(turned_re, width // 2, 1),
                turned_im + pltpu.roll(turned_im, width // 2, 1) * sign,
            )
        )
    return units


def y_inverse(units):
    width = 128
    count = 2 * len(units)
    left, one, zero = lane_consts(width)
    sign = jnp.where(left, one, -one)
    spectrum = [None] * (count // 2 + 1)
    first, middle = units[0]
    spectrum[0] = (first * sign + pltpu.roll(first, width // 2, 1), None)
    spectrum[count // 2] = (middle * (sign + sign), None)
    for k in range(1, count // 2):
        angle = 2 * math.pi * k / (2 * count)
        cos = jnp.where(left, one, math.cos(angle) * one)
        sin = jnp.where(left, zero, math.sin(angle) * one)
        re, im = units[k]
        sum_re = re * sign + pltpu.roll(re, width // 2, 1)
        sum_im = im - pltpu.roll(im, width // 2, 1) * sign
        spectrum[k] = (sum_re * cos - sum_im * sin, sum_im * cos + sum_re * sin)
    return real_inverse(spectrum)


def forward_y_kernel(place_ref, grid_ref, mine_ref, other_ref):
    count = grid_ref.shape[1] // 128
    rows = mine_ref.shape[1]

    def run(low_ref, high_ref):
        def step(tile, carry):
            at = pl.ds(pl.multiple_of(tile * 8, 8), 8)
            units = y_forward(lambda b: grid_ref[at, b * 128 : (b + 1) * 128], count)
            half = len(units) // 2
            for k, (re, im) in enumerate(units):
                out = low_ref if k < half else high_ref
                out[2 * (k % half), at, :] = re
                out[2 * (k % half) + 1, at, :] = im
            return carry

        lax.fori_loop(0, rows // 8, step, 0, unroll=UNROLL)

    @pl.when(place_ref[0] == 0)
    def _():
        run(mine_ref, other_ref)

    @pl.when(place_ref[0] == 1)
    def _():
        run(other_ref, mine_ref)


def forward_y(place, grid):
    rows, width = grid.shape
    out = jax.ShapeDtypeStruct((width // 256, rows, 128), F32)
    return pl.pallas_call(
        forward_y_kernel,
        in_specs=[SMEM, VMEM],
        out_specs=[VMEM, VMEM],
        out_shape=[out, out],
        compiler_params=pltpu.CompilerParams(vmem_limit_bytes=40 * 1024 * 1024),
    )(place, grid)


def forward_rec_kernel(place_ref, grid_ref, mine_ref, other_ref, rows_ref, sems):
    share = mine_ref.shape[1]
    count = grid_ref.shape[1] // 128
    copies = []
    for turn in range(COLORS):
        start = lax.rem(place_ref[1] + turn, COLORS) * 2 * share + place_ref[2] * share
        rows = pl.ds(pl.multiple_of(start, share), share)
        copies.append(pltpu.make_async_copy(grid_ref.at[rows, :], rows_ref.at[turn], sems.at[turn]))
        copies[-1].start()
    for copy in copies:
        copy.wait()

    def run(low_ref, high_ref):
        for turn in range(COLORS):
            for tile in range(share // 8):
                at = pl.ds(tile * 8, 8)
                units = y_forward(lambda b: rows_ref[turn, at, b * 128 : (b + 1) * 128], count)
                half = len(units) // 2
                for piece in range(2 * half):
                    if (2 * (piece // 8) + piece) % COLORS == turn:
                        low_ref[piece, at, :] = units[piece // 2][piece % 2]
                        high_ref[piece, at, :] = units[half + piece // 2][piece % 2]

    @pl.when(place_ref[0] == 0)
    def _():
        run(mine_ref, other_ref)

    @pl.when(place_ref[0] == 1)
    def _():
        run(other_ref, mine_ref)


def forward_rec(place, grid):
    rows, width = grid.shape
    share = rows // (2 * COLORS)
    out = jax.ShapeDtypeStruct((width // 256, share, 128), F32)
    return pl.pallas_call(
        forward_rec_kernel,
        in_specs=[SMEM, pl.BlockSpec(memory_space=pl.ANY)],
        out_specs=[VMEM, VMEM],
        scratch_shapes=[
            pltpu.VMEM((COLORS, share, width), F32),
            pltpu.SemaphoreType.DMA((COLORS,)),
        ],
        out_shape=[out, out],
        compiler_params=pltpu.CompilerParams(vmem_limit_bytes=40 * 1024 * 1024),
    )(place, grid)


def unit_tiles(step, odd, first_re, first_im):
    left = lax.broadcasted_iota(jnp.int32, first_re.shape, 1) < first_re.shape[1] // 2
    mask = jnp.where(left, 1.0 - odd, 0.0)
    rolled = pltpu.roll(first_im, first_im.shape[1] // 2, 1)
    keep = jnp.where(step == 0, odd, 1.0)
    extra = step == STEPS - 1
    re = jnp.where(extra, first_im * mask, first_re)
    im = jnp.where(extra, rolled * mask, first_im * keep)
    return re, im


def signed(table, rows, cols, down, right, both):
    row = lax.broadcasted_iota(jnp.int32, table.shape, 0) // rows % 2 == 0
    col = lax.broadcasted_iota(jnp.int32, table.shape, 1) // cols % 2 == 0
    return table * jnp.where(row, jnp.where(col, 1.0, right), jnp.where(col, down, both))


STEPS = 9
BATCH = 9


def rows_of(lanes):
    grids = [lanes[at : at + 64] for at in range(0, lanes.shape[0], 64)]
    return jnp.concatenate(
        [jnp.concatenate([g[:, k * 128 : (k + 1) * 128] for g in grids], axis=1) for k in range(2)], axis=0
    )


def lanes_of(rows):
    return jnp.concatenate(
        [
            jnp.concatenate([rows[:64, at : at + 128], rows[64:, at : at + 128]], axis=1)
            for at in range(0, rows.shape[1], 128)
        ],
        axis=0,
    )


def spectrum_kernel(place_ref, turn_ref, signs_ref, mine_ref, other_ref, lane_ref, row_ref, out_ref, lane_work):
    place = place_ref[0]
    odd = place.astype(F32)
    channels = mine_ref.shape[1] // 32
    slots = out_ref.shape[0]
    is_low = place == 0

    def tiles(step, c):
        unit = lax.rem(step, STEPS - 1)
        at = pl.ds(c * 32, 32)
        parts = []
        for part in range(2):
            own, far = mine_ref[2 * unit + part, at, :], other_ref[2 * unit + part, at, :]
            parts.append(
                jnp.concatenate([jnp.where(is_low, own, far), jnp.where(is_low, far, own)], axis=0)
            )
        return unit_tiles(step, odd, *parts)

    for slot in range(slots):
        turn = turn_ref[slot]
        sx, sy, sz = (signs_ref[turn, k] for k in range(3))
        row_table = row_stack(signed(row_ref[...], 64, 64, sx, sx, 1.0))

        def run(swapped):
            table = signed(lane_ref[int(swapped)], 64 if swapped else 128, 128, sy * sz, sz, sy)
            lane_work[...] = lane_stack(table)

            def step(count, carry):
                grids = []
                for d in range(BATCH):
                    for c in range(channels):
                        re, im = tiles(count * BATCH + d, c)
                        if swapped:
                            turned = jnp.concatenate([re, im], axis=0).T
                            re, im = turned[:64], turned[64:]
                        grids.append(jnp.concatenate([re, im], axis=1))
                along = lane_dot(jnp.concatenate(grids, axis=0), lane_work[...])
                done = row_dot(row_table, rows_of(along))
                for d in range(BATCH):
                    for c in range(channels):
                        at = (d * channels + c) * 128
                        out_ref[slot, count * BATCH + d, c] = done[:, at : at + 128]
                return carry

            lax.fori_loop(0, STEPS // BATCH, step, 0)

        @pl.when(lax.rem(turn, 2) == 0)
        def _():
            run(False)

        @pl.when(lax.rem(turn, 2) == 1)
        def _():
            run(True)


def spectrum(place, turns, signs, mine, other, lane, row):
    pieces, rows, _ = mine.shape
    slots = turns.shape[0]
    channels = rows // 32
    return pl.pallas_call(
        spectrum_kernel,
        in_specs=[SMEM, SMEM, SMEM, VMEM, VMEM, VMEM, VMEM],
        out_specs=VMEM,
        scratch_shapes=[pltpu.VMEM((768, 256), BF16)],
        out_shape=jax.ShapeDtypeStruct((slots, STEPS, channels, 128, 128), F32),
        compiler_params=pltpu.CompilerParams(vmem_limit_bytes=40 * 1024 * 1024),
    )(place, turns, signs, mine, other, lane, row)


def product_kernel(
    factor, place_ref, own_ref, up_a, up_b, far_a, far_b, down_a, down_b, lig_ref, lane_ref, row_ref,
    mine_ref, other_ref, lane_work, back_work, planes,
):
    place = place_ref[0]
    odd = place.astype(F32)
    slots, steps, channels = lig_ref.shape[:3]
    lane_work[...] = lane_stack(lane_ref[0])
    back_work[...] = lane_stack(signed(lane_ref[0] * factor, 128, 128, -1.0, -1.0, 1.0))
    row_table = row_stack(row_ref[...])
    back_row = row_stack(signed(row_ref[...], 64, 64, -1.0, -1.0, 1.0))
    own = pl.ds(pl.multiple_of(place * 32, 32), 32)
    far = pl.ds(pl.multiple_of(32 - place * 32, 32), 32)
    rest = [(up_a, up_b), (far_a, far_b), (down_a, down_b)]

    def tile(turn, piece):
        if turn == 0:
            ref, at = own_ref, 2 * piece
        else:
            half = own_ref.shape[0] // 4
            ref, at = rest[turn - 1][piece // half], 2 * (piece % half)
        return jnp.concatenate([ref[at + p, s] for s in range(2) for p in range(2)], axis=0)

    grids = []
    for u in range(steps):
        unit = u % (steps - 1)
        for turn in range(channels):
            re, im = unit_tiles(u, odd, tile(turn, 2 * unit), tile(turn, 2 * unit + 1))
            grids.append(jnp.concatenate([re, im], axis=1))
    along = lane_dot(jnp.concatenate(grids, axis=0), lane_work[...])
    rec = row_dot(row_table, rows_of(along))
    sums = []
    for u in range(steps):
        for i in range(slots):
            for turn in range(channels):
                c = lax.rem(place_ref[3] + turn, channels)
                at = (u * channels + turn) * 128
                rec_re, rec_im = rec[:64, at : at + 128], rec[64:, at : at + 128]
                re, im = lig_ref[i, u, c, :64], lig_ref[i, u, c, 64:]
                term = (rec_re * re + rec_im * im, rec_re * im - rec_im * re)
                total = term if turn == 0 else (total[0] + term[0], total[1] + term[1])
            sums.append(jnp.concatenate(total, axis=0))
    rows = row_dot(back_row, jnp.concatenate(sums, axis=1))
    back = lane_dot(lanes_of(rows), back_work[...])
    parts = [back[u * slots * 64 : (u + 1) * slots * 64] for u in range(steps)]
    re, im = parts[-1][:, :128], parts[-1][:, 128:]
    left = lax.broadcasted_iota(jnp.int32, re.shape, 1) < 64
    extra = jnp.where(left, re, pltpu.roll(im, 64, 1))
    for u in range(steps - 1):
        re, im = parts[u][:, :128], parts[u][:, 128:]
        if u == 0:
            im = jnp.where(place == 0, extra, im)
        for part, value in enumerate((re, im)):
            planes[2 * u + part] = value.reshape(slots, 64, 128)
            for i in range(slots):
                mine_ref[2 * u + part, i] = planes[2 * u + part, i, own, :]
                other_ref[2 * u + part, i] = planes[2 * u + part, i, far, :]


def product(place, rec, lig, lane, row, factor):
    slots = lig.shape[0]
    pieces = 2 * (lig.shape[1] - 1)
    out = jax.ShapeDtypeStruct((pieces, slots, 32, 128), F32)
    return pl.pallas_call(
        lambda *refs: product_kernel(factor, *refs),
        in_specs=[SMEM] + [VMEM] * (len(rec) + 3),
        out_specs=[VMEM, VMEM],
        scratch_shapes=[
            pltpu.VMEM((768, 256), BF16),
            pltpu.VMEM((768, 256), BF16),
            pltpu.VMEM((pieces, slots, 64, 128), F32),
        ],
        out_shape=[out, out],
        compiler_params=pltpu.CompilerParams(vmem_limit_bytes=40 * 1024 * 1024),
    )(place, *rec, lig, lane, row)


def inverse_y_kernel(place_ref, mine_ref, other_ref, out_ref):
    pieces, slots, rows, _ = mine_ref.shape
    is_low = place_ref[0] == 0

    def step(tile, carry):
        slot = tile // (rows // 8)
        at = pl.ds(pl.multiple_of(tile % (rows // 8) * 8, 8), 8)
        low, high = [], []
        for k in range(pieces // 2):
            own = [mine_ref[2 * k + part, slot, at, :] for part in range(2)]
            far = [other_ref[2 * k + part, slot, at, :] for part in range(2)]
            low.append(tuple(jnp.where(is_low, a, b) for a, b in zip(own, far)))
            high.append(tuple(jnp.where(is_low, b, a) for a, b in zip(own, far)))
        for b, value in enumerate(y_inverse(low + high)):
            out_ref[slot, at, b * 128 : (b + 1) * 128] = value
        return carry

    lax.fori_loop(0, slots * (rows // 8), step, 0, unroll=UNROLL)


def inverse_y(place, mine, other):
    pieces, slots, rows, _ = mine.shape
    return pl.pallas_call(
        inverse_y_kernel,
        in_specs=[SMEM, VMEM, VMEM],
        out_specs=VMEM,
        out_shape=jax.ShapeDtypeStruct((slots, rows, pieces * 256), F32),
        compiler_params=pltpu.CompilerParams(vmem_limit_bytes=40 * 1024 * 1024),
    )(place, mine, other)


RING_X, RING_Y, RING_Z = 4, 4, 8


def color(x, y, z):
    return (x + 2 * y + z) % COLORS


def color_groups():
    return [
        [
            ((yl * RING_Z + z) * 2 * RING_X + yh * RING_X + (c - color(0, yl, z)) % RING_X) * 2 + core
            for yl in range(2)
            for z in range(RING_Z)
            for yh in range(2)
        ]
        for c in range(COLORS)
        for core in range(2)
    ]


def shift_x(step):
    return [(yh * RING_X + x, yh * RING_X + (x + step) % RING_X) for yh in range(2) for x in range(RING_X)]


def shift_y(step):
    place = lambda y, x: (y % 2) * 2 * RING_X + (y // 2) * RING_X + x
    return [(place(y, x), place((y + step) % RING_Y, x)) for y in range(RING_Y) for x in range(RING_X)]


def shift_z(step):
    return [(z, (z + step) % RING_Z) for z in range(RING_Z)]


def per_device(receptors, ligands, plan, rotations):
    _, channels, half, flat = ligands.shape
    length = 2 * half
    core = lax.axis_index("slab")
    y_hi, x = lax.axis_index("lig") // RING_X, lax.axis_index("lig") % RING_X
    tone = color(x, lax.axis_index("yl"), lax.axis_index("z"))
    place = jnp.stack([core, x, y_hi, tone]).astype(jnp.int32)
    swap = lambda value: lax.ppermute(value, "slab", [(0, 1), (1, 0)])
    lane, row = (jnp.asarray(table) for table in base_tables(length))
    signs = jnp.asarray(SIGNS)
    factor = 1.0 / (math.sqrt(channels * length**3) * length**3)

    rec_mine, rec_other = forward_rec(place, receptors.reshape(channels * half, flat))
    rec_far = swap(rec_other)
    is_low = core == 0
    rec_share = jnp.stack(
        [jnp.where(is_low, rec_mine, rec_far), jnp.where(is_low, rec_far, rec_mine)], axis=1
    )
    scattered = lax.all_to_all(rec_share, ("yl", "z"), split_axis=0, concat_axis=0)
    piece = lax.dynamic_index_in_dim(scattered, plan[0], 0, True)

    lig_mine, lig_other = forward_y(place, ligands.reshape(channels * half, flat))
    lig_far = swap(lig_other)
    piece, lig_mine, lig_far = lax.optimization_barrier((piece, lig_mine, lig_far))

    groups = color_groups()
    block = lax.all_to_all(
        jnp.broadcast_to(piece, (len(groups[0]), *piece.shape[1:])),
        ("yl", "z", "lig", "slab"),
        split_axis=0,
        concat_axis=0,
        axis_index_groups=groups,
    )
    block, lig_mine, lig_far = lax.optimization_barrier((block, lig_mine, lig_far))
    first, second = jnp.split(block, 2)
    rec = [
        block,
        lax.ppermute(first, "lig", shift_x(-1)),
        lax.ppermute(second, "z", shift_z(-1)),
        lax.ppermute(first, ("yl", "lig"), shift_y(1)),
        lax.ppermute(second, ("yl", "lig"), shift_y(-1)),
        lax.ppermute(first, "lig", shift_x(1)),
        lax.ppermute(second, "z", shift_z(1)),
    ]
    lig_spec = spectrum(place, rotations, signs, lig_mine, lig_far, lane, row)

    out_mine, out_other = product(place, rec, lig_spec, lane, row, factor)
    out_far = swap(out_other)
    scores = inverse_y(place, out_mine, out_far)
    return scores[None, :, None]


def solution(mesh):
    fine = Mesh(mesh.devices.reshape(2, RING_Z, 2 * RING_X, 2), ("yl", "z", "lig", "slab"))
    return jax.shard_map(
        per_device,
        mesh=fine,
        in_specs=(P(("yl", "z"), None, "slab", None), P(("yl", "z", "lig"), None, "slab", None), P(), P()),
        out_specs=P(None, None, ("yl", "z", "lig"), "slab", None),
        check_vma=False,
    )
```

time: 102 us -> 79.7 us (0.78); the launches traced: 100 us -> 79.5 us
  Pallas kernels: 44.7 us -> 16.6 us
  blocking collectives: 13.1 us -> 26.7 us
  waiting for transfers between devices: 13.7 us -> 10.2 us
  local copies, waits for them, and re-layouts: 5.54 us -> 2.43 us
  starting transfers between devices: 21.1 us -> 22.7 us
  other arithmetic: 1.53 us -> 0.12 us
    pallas_call x5, Pallas kernels: 44.7 us -> 16.6 us  [the longest x1 5.87 us: spectrum(): pl.pallas_call(spectrum_kernel, in_specs=[SMEM, SMEM, SMEM, VMEM, VMEM, V...]
    all_to_all x1, blocking collectives: 13.1 us -> 26.7 us  [per_device(): lax.all_to_all(jnp.broadcast_to(piece, (len(groups[0]), *piece.shape[1:])...]
    ppermute x0 -> x6, starting transfers between devices: none -> 6.97 us  [the longest x1 2.59 us: per_device(): lax.ppermute(second, ('yl', 'lig'), shift_y(-1))]
    all_to_all x2 -> x1, starting transfers between devices: 13.9 us -> 7.57 us  [per_device(): lax.all_to_all(rec_share, ('yl', 'z'), split_axis=0, concat_axis=0)]
    ppermute x3, waiting for transfers between devices: 5.44 us -> 1.54 us  [per_device(): swap = lambda value: lax.ppermute(value, 'slab', [(0, 1), (1, 0)])]
    broadcast_in_dim x3 -> x1, local copies, waits for them, and re-layouts: 1.67 us -> 0.05 us  [per_device(): jnp.broadcast_to(piece, (len(groups[0]), *piece.shape[1:]))]
    unnamed x6 -> x12, local copies, waits for them, and re-layouts: 3.15 us -> 1.62 us
    all_to_all x2 -> x1, waiting for transfers between devices: 8.31 us -> 8.62 us  [per_device(): lax.all_to_all(rec_share, ('yl', 'z'), split_axis=0, concat_axis=0)]
  transfers between devices with their start and end apart: 5 -> 10, of which waited for: 4 -> 2; matrix products, arithmetic and copies ran while one was open for 0% -> 1% of each run, Pallas kernels for 25% -> 11%
where the time goes in v1:
time: 79.7 us; the launch traced here: 79.5 us
  blocking collectives  26.7 us (34%)
  starting transfers between devices  22.7 us (28%)
  Pallas kernels  16.6 us (21%)
  waiting for transfers between devices  10.2 us (13%)
  local copies, waits for them, and re-layouts  2.43 us (3%)
  between operations  0.8 us (1%)
    all_to_all x1, blocking collectives, per_device(): lax.all_to_all(jnp.broadcast_to(piece, (len(groups[0]), *piece.shape[1:])...  26.7 us
    all_to_all x1, waiting for transfers between devices, per_device(): lax.all_to_all(rec_share, ('yl', 'z'), split_axis=0, concat_axis=0)  8.62 us
    ppermute x3, starting transfers between devices, per_device(): swap = lambda value: lax.ppermute(value, 'slab', [(0, 1), (1, 0)])  8.13 us
    all_to_all x1, starting transfers between devices, per_device(): lax.all_to_all(rec_share, ('yl', 'z'), split_axis=0, concat_axis=0)  7.57 us
    pallas_call x1, Pallas kernels, spectrum(): pl.pallas_call(spectrum_kernel, in_specs=[SMEM, SMEM, SMEM, VMEM, VMEM, V...  5.87 us
    pallas_call x1, Pallas kernels, product(): pl.pallas_call(lambda *refs: product_kernel(factor, *refs), in_specs=[SME...  4.83 us
    pallas_call x1, Pallas kernels, forward_y(): pl.pallas_call(forward_y_kernel, in_specs=[SMEM, VMEM], out_specs=[VMEM,...  2.7 us
    ppermute x1, starting transfers between devices, per_device(): lax.ppermute(second, ('yl', 'lig'), shift_y(-1))  2.59 us
  transfers between devices with their start and end apart: 10, of which 2 were waited for; matrix products, arithmetic and copies ran while one was open for 1% of the time, Pallas kernels for 11%

profile of v1, /device:TPU:1, one launch (start us, length us, event | category | flops | bytes accessed | tf_op | source)
XLA Modules:
  0.0 79.5 jit_solution(15622903304718074304)
XLA Ops:
  0.0 0.1 pad_add_fusion.place_ref.refs_0_
  0.1 1.6 %copy-done.1 = f32[1,4,32,4096]{3,2,1,0:T(8,128)S(1)} copy-done((f32[1,4,32,4096]{3,2,1,0:T(8,128)S(1)}, f32[1,4,32,4096]{3,2,1,0:T(8,128)}, u32[]{:S(2)}) %copy-start.1) | copy-done | bytes 2097176
  1.7 1.0 %shard_map.73 = (f32[16,16,128]{2,1,0:T(8,128)S(1)}, f32[16,16,128]{2,1,0:T(8,128)S(1)}) custom-call(s32[4]{0:T(128)S(1)} %pad_add_fusion.place_ref.refs_0_, f32[128,4096]{1,0:T(8,128)S(1)} %bitcast.18), custom_call_target="tpu_custom_call" | custom-call | tf_op jit(solution)/shard_map/pallas_call | solution.py:250
  2.7 3.3 %collective-permute-start = (f32[16,16,128]{2,1,0:T(8,128)S(1)}, f32[16,16,128]{2,1,0:T(8,128)S(1)}, u32[]{:S(2)}, u32[]{:S(2)}) collective-permute-start(f32[16,16,128]{2,1,0:T(8,128)S(1)} %get-tuple-element.18), channel_id=1, source_target_pairs={{0,1},{1,0},{2,3},{3,2},{4,5},{5,4},{6,7},{7,6},{8,9},{9,8},{10,11... | collective-permute-start | bytes 393224 | tf_op jit(solution)/shard_map/ppermute | solution.py:518
  6.0 2.7 %shard_map.74 = (f32[16,128,128]{2,1,0:T(8,128)S(1)}, f32[16,128,128]{2,1,0:T(8,128)}) custom-call(s32[4]{0:T(128)S(1)} %pad_add_fusion.place_ref.refs_0_, f32[128,4096]{1,0:T(8,128)S(1)} %bitcast.19), custom_call_target="tpu_custom_call" | custom-call | tf_op jit(solution)/shard_map/pallas_call | solution.py:205
  8.7 0.5 collective-permute-start.1
  9.2 0.0 copy-start
  9.2 0.0 copy-start.3
  9.3 0.0 copy-start.4
  9.3 0.7 copy.9
  10.0 7.6 %all-to-all-start = ((f32[16,2,16,128]{3,2,1,0:T(8,128)}), f32[16,2,16,128]{3,2,1,0:T(8,128)S(1)}, u32[]{:S(2)}, u32[]{:S(2)}) async-start(f32[16,2,16,128]{3,2,1,0:T(8,128)} %copy.9), calls=%async_computation | async-start | bytes 524288 | tf_op jit(solution)/shard_map/all_to_all | solution.py:529
  18.3 8.6 %all-to-all-done = f32[16,2,16,128]{3,2,1,0:T(8,128)S(1)} async-done(((f32[16,2,16,128]{3,2,1,0:T(8,128)}), f32[16,2,16,128]{3,2,1,0:T(8,128)S(1)}, u32[]{:S(2)}, u32[]{:S(2)}) %all-to-all-start) | async-done | bytes 262176 | tf_op jit(solution)/shard_map/all_to_all | solution.py:529
  26.9 0.1 broadcast_in_dim.11
  26.9 26.7 %all_to_all.10.refs_1_ = f32[32,2,16,128]{3,2,1,0:T(8,128)S(1)} all-to-all(f32[32,2,16,128]{3,2,1,0:T(8,128)S(1)} %broadcast_in_dim.11), channel_id=1, replica_groups={{0,8,22,30,36,44,50,58,64,72,86,94,100,108,114,122,132,140,146,154,160,..., dimensions={0} | all-to-all | bytes 1048576 | tf_op jit(solution)/shard_map/all_to_all | solution.py:537
  53.7 0.8 collective-permute-start.2
  54.4 1.0 %collective-permute-start.3 = (f32[16,2,16,128]{3,2,1,0:T(8,128)S(1)}, f32[16,2,16,128]{3,2,1,0:T(8,128)S(1)}, u32[]{:S(2)}, u32[]{:S(2)}) collective-permute-start(f32[16,2,16,128]{3,2,1,0:T(8,128)S(1)} %get-tuple-element.29), channel_id=1, source_target_pairs={{0,112},{16,0},{32,16},{48,32},{64,48},{80,64},{96,80},{112,96},{1... | collective-permute-start | bytes 786440 | tf_op jit(solution)/shard_map/ppermute | solution.py:549
  55.5 2.6 %collective-permute-start.5 = (f32[16,2,16,128]{3,2,1,0:T(8,128)S(1)}, f32[16,2,16,128]{3,2,1,0:T(8,128)S(1)}, u32[]{:S(2)}, u32[]{:S(2)}) collective-permute-start(f32[16,2,16,128]{3,2,1,0:T(8,128)S(1)} %get-tuple-element.29), channel_id=1, source_target_pairs={{0,136},{2,138},{4,140},{6,142},{128,0},{130,2},{132,4},{134,6},{8... | collective-permute-start | bytes 786440 | tf_op jit(solution)/shard_map/ppermute | solution.py:551
  58.0 1.4 %collective-permute-start.6 = (f32[16,2,16,128]{3,2,1,0:T(8,128)S(1)}, f32[16,2,16,128]{3,2,1,0:T(8,128)S(1)}, u32[]{:S(2)}, u32[]{:S(2)}) collective-permute-start(f32[16,2,16,128]{3,2,1,0:T(8,128)S(1)} %get-tuple-element.30), channel_id=1, source_target_pairs={{0,2},{2,4},{4,6},{6,0},{8,10},{10,12},{12,14},{14,8},{1,3},{3,5},... | collective-permute-start | bytes 786440 | tf_op jit(solution)/shard_map/ppermute | solution.py:552
  59.4 1.2 %collective-permute-start.7 = (f32[16,2,16,128]{3,2,1,0:T(8,128)S(1)}, f32[16,2,16,128]{3,2,1,0:T(8,128)S(1)}, u32[]{:S(2)}, u32[]{:S(2)}) collective-permute-start(f32[16,2,16,128]{3,2,1,0:T(8,128)S(1)} %get-tuple-element.29), channel_id=1, source_target_pairs={{0,16},{16,32},{32,48},{48,64},{64,80},{80,96},{96,112},{112,0},{1... | collective-permute-start | bytes 786440 | tf_op jit(solution)/shard_map/ppermute | solution.py:553
  60.7 5.9 %shard_map.75.refs_8_ = f32[2,9,4,128,128]{4,3,2,1,0:T(8,128)S(1)} custom-call(s32[4]{0:T(128)S(1)} %pad_add_fusion.place_ref.refs_0_, s32[2]{0:T(128)S(1)} %copy-done.5, f32[8,3]{1,0:T(8,128)S(1)} %copy-done.4, f32[16,128,128]{2,1,0:T(8,128)S(1)} %get-tuple-element.25.mine_ref, f32[16,128,128]{2,1,0:T(8,128)S(1)} %collective-permute-done.1.other_ref, ...), custom_call_target="tpu_custom_call" | custom-call | tf_op jit(solution)/shard_map/pallas_call | solution.py:360
  66.6 4.8 %shard_map.76 = (f32[16,2,32,128]{3,2,1,0:T(8,128)S(1)}, f32[16,2,32,128]{3,2,1,0:T(8,128)S(1)}) custom-call(s32[4]{0:T(128)S(1)} %pad_add_fusion.place_ref.refs_0_, f32[32,2,16,128]{3,2,1,0:T(8,128)S(1)} %all_to_all.10.refs_1_, f32[16,2,16,128]{3,2,1,0:T(8,128)S(1)} %collective-permute-done.2.refs_2_, ...), custom_call_target="tpu_custom_call" | custom-call | tf_op jit(solution)/shard_map/pallas_call | solution.py:433
  71.4 4.4 %collective-permute-start.8 = (f32[16,2,32,128]{3,2,1,0:T(8,128)S(1)}, f32[16,2,32,128]{3,2,1,0:T(8,128)S(1)}, u32[]{:S(2)}, u32[]{:S(2)}) collective-permute-start(f32[16,2,32,128]{3,2,1,0:T(8,128)S(1)} %get-tuple-element.28), channel_id=1, source_target_pairs={{0,1},{1,0},{2,3},{3,2},{4,5},{5,4},{6,7},{7,6},{8,9},{9,8},{10,11... | collective-permute-start | bytes 1572872 | tf_op jit(solution)/shard_map/ppermute | solution.py:518
  75.8 1.5 %collective-permute-done.8.other_ref = f32[16,2,32,128]{3,2,1,0:T(8,128)S(1)} collective-permute-done((f32[16,2,32,128]{3,2,1,0:T(8,128)S(1)}, f32[16,2,32,128]{3,2,1,0:T(8,128)S(1)}, u32[]{:S(2)}, u32[]{:S(2)}) %collective-permute-start.8) | collective-permute-done | bytes 524320 | tf_op jit(solution)/shard_map/ppermute | solution.py:518
  77.3 2.2 %shard_map.77 = f32[2,32,4096]{2,1,0:T(8,128)} custom-call(s32[4]{0:T(128)S(1)} %pad_add_fusion.place_ref.refs_0_, f32[16,2,32,128]{3,2,1,0:T(8,128)S(1)} %get-tuple-element.27.mine_ref, f32[16,2,32,128]{3,2,1,0:T(8,128)S(1)} %collective-permute-done.8.other_ref), custom_call_target="tpu_custom_call" | custom-call | tf_op jit(solution)/shard_map/pallas_call | solution.py:469
  (21 shorter events, 0.1 us)
Async XLA Ops:
  0.1 1.6 %copy-start.1 = (f32[1,4,32,4096]{3,2,1,0:T(8,128)S(1)}, f32[1,4,32,4096]{3,2,1,0:T(8,128)}, u32[]{:S(2)}) copy-start(f32[1,4,32,4096]{3,2,1,0:T(8,128)} %param.7) | copy-start | bytes 6291460
  1.7 4.4 %copy-start.2 = (f32[1,4,32,4096]{3,2,1,0:T(8,128)S(1)}, f32[1,4,32,4096]{3,2,1,0:T(8,128)}, u32[]{:S(2)}) copy-start(f32[1,4,32,4096]{3,2,1,0:T(8,128)} %param.8) | copy-start | bytes 6291460
  2.7 6.5 %collective-permute-start = (f32[16,16,128]{2,1,0:T(8,128)S(1)}, f32[16,16,128]{2,1,0:T(8,128)S(1)}, u32[]{:S(2)}, u32[]{:S(2)}) collective-permute-start(f32[16,16,128]{2,1,0:T(8,128)S(1)} %get-tuple-element.18), channel_id=1, source_target_pairs={{0,1},{1,0},{2,3},{3,2},{4,5},{5,4},{6,7},{7,6},{8,9},{9,8},{10,11... | collective-permute-start | bytes 393224 | tf_op jit(solution)/shard_map/ppermute | solution.py:518
  8.7 18.1 %collective-permute-start.1 = (f32[16,128,128]{2,1,0:T(8,128)}, f32[16,128,128]{2,1,0:T(8,128)S(1)}, u32[]{:S(2)}, u32[]{:S(2)}) collective-permute-start(f32[16,128,128]{2,1,0:T(8,128)} %get-tuple-element.20), channel_id=1, source_target_pairs={{0,1},{1,0},{2,3},{3,2},{4,5},{5,4},{6,7},{7,6},{8,9},{9,8},{10,11... | collective-permute-start | bytes 3145736 | tf_op jit(solution)/shard_map/ppermute | solution.py:518
  9.2 51.4 %copy-start = (f32[2,256,256]{2,1,0:T(8,128)S(1)}, f32[2,256,256]{2,1,0:T(8,128)}, u32[]{:S(2)}) copy-start(f32[2,256,256]{2,1,0:T(8,128)} %constant.58.clone.lane_ref.refs_9_) | copy-start | bytes 1572868
  9.2 51.4 %copy-start.3 = (f32[128,128]{1,0:T(8,128)S(1)}, f32[128,128]{1,0:T(8,128)}, u32[]{:S(2)}) copy-start(f32[128,128]{1,0:T(8,128)} %constant.59.clone.row_ref.refs_10_) | copy-start | bytes 196612
  9.3 51.4 %copy-start.4 = (f32[8,3]{1,0:T(8,128)S(1)}, f32[8,3]{1,0:T(8,128)}, u32[]{:S(2)}) copy-start(f32[8,3]{1,0:T(8,128)} %constant.60.clone.signs_ref) | copy-start | bytes 292
  9.3 51.4 %copy-start.5 = (s32[2]{0:T(128)S(1)}, s32[2]{0:T(128)}, u32[]{:S(2)}) copy-start(s32[2]{0:T(128)} %turn_ref.1) | copy-start | bytes 28
  10.0 16.8 %all-to-all-start = ((f32[16,2,16,128]{3,2,1,0:T(8,128)}), f32[16,2,16,128]{3,2,1,0:T(8,128)S(1)}, u32[]{:S(2)}, u32[]{:S(2)}) async-start(f32[16,2,16,128]{3,2,1,0:T(8,128)} %copy.9), calls=%async_computation | async-start | bytes 524288 | tf_op jit(solution)/shard_map/all_to_all | solution.py:529
  53.7 5.8 %collective-permute-start.2 = (f32[16,2,16,128]{3,2,1,0:T(8,128)S(1)}, f32[16,2,16,128]{3,2,1,0:T(8,128)S(1)}, u32[]{:S(2)}, u32[]{:S(2)}) collective-permute-start(f32[16,2,16,128]{3,2,1,0:T(8,128)S(1)} %get-tuple-element.30), channel_id=1, source_target_pairs={{0,6},{2,0},{4,2},{6,4},{8,14},{10,8},{12,10},{14,12},{1,7},{3,1},... | collective-permute-start | bytes 786440 | tf_op jit(solution)/shard_map/ppermute | solution.py:548
  54.4 12.1 %collective-permute-start.4 = (f32[16,2,16,128]{3,2,1,0:T(8,128)S(1)}, f32[16,2,16,128]{3,2,1,0:T(8,128)S(1)}, u32[]{:S(2)}, u32[]{:S(2)}) collective-permute-start(f32[16,2,16,128]{3,2,1,0:T(8,128)S(1)} %get-tuple-element.30), channel_id=1, source_target_pairs={{0,128},{2,130},{4,132},{6,134},{128,8},{130,10},{132,12},{134,14}... | collective-permute-start | bytes 786440 | tf_op jit(solution)/shard_map/ppermute | solution.py:550
  54.4 12.1 %collective-permute-start.3 = (f32[16,2,16,128]{3,2,1,0:T(8,128)S(1)}, f32[16,2,16,128]{3,2,1,0:T(8,128)S(1)}, u32[]{:S(2)}, u32[]{:S(2)}) collective-permute-start(f32[16,2,16,128]{3,2,1,0:T(8,128)S(1)} %get-tuple-element.29), channel_id=1, source_target_pairs={{0,112},{16,0},{32,16},{48,32},{64,48},{80,64},{96,80},{112,96},{1... | collective-permute-start | bytes 786440 | tf_op jit(solution)/shard_map/ppermute | solution.py:549
  55.5 11.1 %collective-permute-start.5 = (f32[16,2,16,128]{3,2,1,0:T(8,128)S(1)}, f32[16,2,16,128]{3,2,1,0:T(8,128)S(1)}, u32[]{:S(2)}, u32[]{:S(2)}) collective-permute-start(f32[16,2,16,128]{3,2,1,0:T(8,128)S(1)} %get-tuple-element.29), channel_id=1, source_target_pairs={{0,136},{2,138},{4,140},{6,142},{128,0},{130,2},{132,4},{134,6},{8... | collective-permute-start | bytes 786440 | tf_op jit(solution)/shard_map/ppermute | solution.py:551
  58.0 8.5 %collective-permute-start.6 = (f32[16,2,16,128]{3,2,1,0:T(8,128)S(1)}, f32[16,2,16,128]{3,2,1,0:T(8,128)S(1)}, u32[]{:S(2)}, u32[]{:S(2)}) collective-permute-start(f32[16,2,16,128]{3,2,1,0:T(8,128)S(1)} %get-tuple-element.30), channel_id=1, source_target_pairs={{0,2},{2,4},{4,6},{6,0},{8,10},{10,12},{12,14},{14,8},{1,3},{3,5},... | collective-permute-start | bytes 786440 | tf_op jit(solution)/shard_map/ppermute | solution.py:552
  59.4 7.2 %collective-permute-start.7 = (f32[16,2,16,128]{3,2,1,0:T(8,128)S(1)}, f32[16,2,16,128]{3,2,1,0:T(8,128)S(1)}, u32[]{:S(2)}, u32[]{:S(2)}) collective-permute-start(f32[16,2,16,128]{3,2,1,0:T(8,128)S(1)} %get-tuple-element.29), channel_id=1, source_target_pairs={{0,16},{16,32},{32,48},{48,64},{64,80},{80,96},{96,112},{112,0},{1... | collective-permute-start | bytes 786440 | tf_op jit(solution)/shard_map/ppermute | solution.py:553
  71.4 5.9 %collective-permute-start.8 = (f32[16,2,32,128]{3,2,1,0:T(8,128)S(1)}, f32[16,2,32,128]{3,2,1,0:T(8,128)S(1)}, u32[]{:S(2)}, u32[]{:S(2)}) collective-permute-start(f32[16,2,32,128]{3,2,1,0:T(8,128)S(1)} %get-tuple-element.28), channel_id=1, source_target_pairs={{0,1},{1,0},{2,3},{3,2},{4,5},{5,4},{6,7},{7,6},{8,9},{9,8},{10,11... | collective-permute-start | bytes 1572872 | tf_op jit(solution)/shard_map/ppermute | solution.py:518

commit v2 on v1

--- a/solution.py
+++ b/solution.py
@@ -207,57 +207,56 @@
         in_specs=[SMEM, VMEM],
         out_specs=[VMEM, VMEM],
         out_shape=[out, out],
+        cost_estimate=pl.CostEstimate(flops=3 * 10**9, bytes_accessed=4 * 10**6, transcendentals=0),
         compiler_params=pltpu.CompilerParams(vmem_limit_bytes=40 * 1024 * 1024),
     )(place, grid)
 
 
-def forward_rec_kernel(place_ref, grid_ref, mine_ref, other_ref, rows_ref, sems):
-    share = mine_ref.shape[1]
+RING_X, RING_Y, RING_Z = 4, 4, 8
+
+
+def forward_rec_kernel(grid_ref, out_ref, rows_ref, sems):
+    place = lax.axis_index("slab")
+    y_hi, x = lax.axis_index("lig") // RING_X, lax.axis_index("lig") % RING_X
+    share = out_ref.shape[2]
     count = grid_ref.shape[1] // 128
     copies = []
     for turn in range(COLORS):
-        start = lax.rem(place_ref[1] + turn, COLORS) * 2 * share + place_ref[2] * share
+        start = lax.rem(x + turn, COLORS) * 2 * share + y_hi * share
         rows = pl.ds(pl.multiple_of(start, share), share)
         copies.append(pltpu.make_async_copy(grid_ref.at[rows, :], rows_ref.at[turn], sems.at[turn]))
         copies[-1].start()
-    for copy in copies:
-        copy.wait()
-
-    def run(low_ref, high_ref):
-        for turn in range(COLORS):
-            for tile in range(share // 8):
-                at = pl.ds(tile * 8, 8)
-                units = y_forward(lambda b: rows_ref[turn, at, b * 128 : (b + 1) * 128], count)
-                half = len(units) // 2
-                for piece in range(2 * half):
-                    if (2 * (piece // 8) + piece) % COLORS == turn:
-                        low_ref[piece, at, :] = units[piece // 2][piece % 2]
-                        high_ref[piece, at, :] = units[half + piece // 2][piece % 2]
-
-    @pl.when(place_ref[0] == 0)
-    def _():
-        run(mine_ref, other_ref)
-
-    @pl.when(place_ref[0] == 1)
-    def _():
-        run(other_ref, mine_ref)
-
-
-def forward_rec(place, grid):
+    def run(turn, core):
+        for tile in range(share // 8):
+            at = pl.ds(tile * 8, 8)
+            units = y_forward(lambda b: rows_ref[turn, at, b * 128 : (b + 1) * 128], count)
+            half = len(units) // 2
+            for piece in range(2 * half):
+                if (2 * (piece // 8) + piece) % COLORS == turn:
+                    for side in range(2):
+                        out_ref[piece, side ^ core, at, :] = units[half * side + piece // 2][piece % 2]
+
+    for turn in range(COLORS):
+        copies[turn].wait()
+        for core in range(2):
+            pl.when(place == core)(lambda turn=turn, core=core: run(turn, core))
+
+
+def forward_rec(grid):
     rows, width = grid.shape
     share = rows // (2 * COLORS)
-    out = jax.ShapeDtypeStruct((width // 256, share, 128), F32)
+    out = jax.ShapeDtypeStruct((width // 256, 2, share, 128), F32)
     return pl.pallas_call(
         forward_rec_kernel,
-        in_specs=[SMEM, pl.BlockSpec(memory_space=pl.ANY)],
-        out_specs=[VMEM, VMEM],
+        in_specs=[pl.BlockSpec(memory_space=pltpu.HBM)],
+        out_specs=VMEM,
         scratch_shapes=[
             pltpu.VMEM((COLORS, share, width), F32),
             pltpu.SemaphoreType.DMA((COLORS,)),
         ],
-        out_shape=[out, out],
-        compiler_params=pltpu.CompilerParams(vmem_limit_bytes=40 * 1024 * 1024),
-    )(place, grid)
+        out_shape=out,
+        compiler_params=pltpu.CompilerParams(vmem_limit_bytes=60 * 1024 * 1024),
+    )(grid)
 
 
 def unit_tiles(step, odd, first_re, first_im):
@@ -363,6 +362,7 @@
         out_specs=VMEM,
         scratch_shapes=[pltpu.VMEM((768, 256), BF16)],
         out_shape=jax.ShapeDtypeStruct((slots, STEPS, channels, 128, 128), F32),
+        cost_estimate=pl.CostEstimate(flops=6 * 10**9, bytes_accessed=7 * 10**6, transcendentals=0),
         compiler_params=pltpu.CompilerParams(vmem_limit_bytes=40 * 1024 * 1024),
     )(place, turns, signs, mine, other, lane, row)
 
@@ -388,7 +388,7 @@
         else:
             half = own_ref.shape[0] // 4
             ref, at = rest[turn - 1][piece // half], 2 * (piece % half)
-        return jnp.concatenate([ref[at + p, s] for s in range(2) for p in range(2)], axis=0)
+        return jnp.concatenate([ref[at + p, s ^ place] for s in range(2) for p in range(2)], axis=0)
 
     grids = []
     for u in range(steps):
@@ -475,9 +475,6 @@
     )(place, mine, other)
 
 
-RING_X, RING_Y, RING_Z = 4, 4, 8
-
-
 def color(x, y, z):
     return (x + 2 * y + z) % COLORS
 
@@ -520,18 +517,16 @@
     signs = jnp.asarray(SIGNS)
     factor = 1.0 / (math.sqrt(channels * length**3) * length**3)
 
-    rec_mine, rec_other = forward_rec(place, receptors.reshape(channels * half, flat))
-    rec_far = swap(rec_other)
-    is_low = core == 0
-    rec_share = jnp.stack(
-        [jnp.where(is_low, rec_mine, rec_far), jnp.where(is_low, rec_far, rec_mine)], axis=1
-    )
+    rec_share = forward_rec(receptors.reshape(channels * half, flat))
+    rec_share, root = lax.optimization_barrier((rec_share, plan[0].astype(jnp.uint32)))
     scattered = lax.all_to_all(rec_share, ("yl", "z"), split_axis=0, concat_axis=0)
-    piece = lax.dynamic_index_in_dim(scattered, plan[0], 0, True)
-
+    scattered, ligands = lax.optimization_barrier((scattered, ligands))
+    piece = lax.dynamic_index_in_dim(scattered, root, 0, False)
+    piece_far = swap(piece[1])
     lig_mine, lig_other = forward_y(place, ligands.reshape(channels * half, flat))
+    piece_far, lig_mine, lig_other = lax.optimization_barrier((piece_far, lig_mine, lig_other))
     lig_far = swap(lig_other)
-    piece, lig_mine, lig_far = lax.optimization_barrier((piece, lig_mine, lig_far))
+    piece = jnp.stack([piece[0], piece_far])[None]
 
     groups = color_groups()
     block = lax.all_to_all(

time: 79.7 us -> 78.4 us (0.984)
  local copies, waits for them, and re-layouts: 2.43 us -> 0.12 us
    all_to_all x1, starting transfers between devices: 7.57 us -> 10.1 us  [per_device(): lax.all_to_all(rec_share, ('yl', 'z'), split_axis=0, concat_axis=0)]
    ppermute x3, starting transfers between devices: 8.13 us -> 6.12 us  [per_device(): swap = lambda value: lax.ppermute(value, 'slab', [(0, 1), (1, 0)])]
    unnamed x12 -> x10, local copies, waits for them, and re-layouts: 1.62 us -> 0.03 us
    pallas_call x1, Pallas kernels: 1.04 us -> 2.41 us  [forward_rec(): pl.pallas_call(forward_rec_kernel, in_specs=[pl.BlockSpec(memory_space=pl...]
    pallas_call x1, Pallas kernels: 2.7 us -> 1.7 us  [forward_y(): pl.pallas_call(forward_y_kernel, in_specs=[SMEM, VMEM], out_specs=[VMEM,...]
  transfers between devices with their start and end apart: 10 -> 10, of which waited for: 2 -> 2; matrix products, arithmetic and copies ran while one was open for 1% -> 0% of each run, Pallas kernels for 11% -> 10%
where the time goes in v2:
time: 78.4 us; the launch traced here: 78.2 us
  blocking collectives  27.1 us (35%)
  starting transfers between devices  23.1 us (29%)
  Pallas kernels  16.8 us (21%)
  waiting for transfers between devices  10.2 us (13%)
  between operations  0.85 us (1%)
    all_to_all x1, blocking collectives, per_device(): lax.all_to_all(jnp.broadcast_to(piece, (len(groups[0]), *piece.shape[1:])...  27.1 us
    all_to_all x1, starting transfers between devices, per_device(): lax.all_to_all(rec_share, ('yl', 'z'), split_axis=0, concat_axis=0)  10.1 us
    all_to_all x1, waiting for transfers between devices, per_device(): lax.all_to_all(rec_share, ('yl', 'z'), split_axis=0, concat_axis=0)  8.61 us
    ppermute x3, starting transfers between devices, per_device(): swap = lambda value: lax.ppermute(value, 'slab', [(0, 1), (1, 0)])  6.12 us
    pallas_call x1, Pallas kernels, spectrum(): pl.pallas_call(spectrum_kernel, in_specs=[SMEM, SMEM, SMEM, VMEM, VMEM, V...  5.82 us
    pallas_call x1, Pallas kernels, product(): pl.pallas_call(lambda *refs: product_kernel(factor, *refs), in_specs=[SME...  4.7 us
    ppermute x1, starting transfers between devices, per_device(): lax.ppermute(second, ('yl', 'lig'), shift_y(-1))  2.57 us
    pallas_call x1, Pallas kernels, forward_rec(): pl.pallas_call(forward_rec_kernel, in_specs=[pl.BlockSpec(memory_space=pl...  2.41 us
  transfers between devices with their start and end apart: 10, of which 2 were waited for; matrix products, arithmetic and copies ran while one was open for 0% of the time, Pallas kernels for 10%

profile of v2, /device:TPU:1, one launch (start us, length us, event | category | flops | bytes accessed | tf_op | source)
XLA Modules:
  0.0 78.2 jit_solution(6225066804028461995)
XLA Ops:
  0.0 2.4 %shard_map.73 = f32[16,2,16,128]{3,2,1,0:T(8,128)} custom-call(f32[128,4096]{1,0:T(8,128)} %bitcast.16), custom_call_target="tpu_custom_call" | custom-call | tf_op jit(solution)/shard_map/pallas_call | solution.py:249
  3.1 10.1 %all-to-all-start = ((f32[16,2,16,128]{3,2,1,0:T(8,128)}), f32[16,2,16,128]{3,2,1,0:T(8,128)S(1)}, u32[]{:S(2)}, u32[]{:S(2)}) async-start(f32[16,2,16,128]{3,2,1,0:T(8,128)} %shard_map.73), calls=%async_computation | async-start | bytes 524288 | tf_op jit(solution)/shard_map/all_to_all | solution.py:522
  13.3 0.1 pad_add_fusion.place_ref.refs_0_
  13.3 8.6 %all-to-all-done = f32[16,2,16,128]{3,2,1,0:T(8,128)S(1)} async-done(((f32[16,2,16,128]{3,2,1,0:T(8,128)}), f32[16,2,16,128]{3,2,1,0:T(8,128)S(1)}, u32[]{:S(2)}, u32[]{:S(2)}) %all-to-all-start) | async-done | bytes 262176 | tf_op jit(solution)/shard_map/all_to_all | solution.py:522
  21.9 2.3 %collective-permute-start = (f32[16,128]{1,0:T(8,128)S(1)}, f32[16,128]{1,0:T(8,128)S(1)}, u32[]{:S(2)}, u32[]{:S(2)}) collective-permute-start(f32[16,128]{1,0:T(8,128)S(1)} %get-tuple-element.36), channel_id=1, source_target_pairs={{0,1},{1,0},{2,3},{3,2},{4,5},{5,4},{6,7},{7,6},{8,9},{9,8},{10,11... | collective-permute-start | bytes 24584 | tf_op jit(solution)/shard_map/ppermute | solution.py:515
  24.3 1.7 %shard_map.74 = (f32[16,128,128]{2,1,0:T(8,128)S(1)}, f32[16,128,128]{2,1,0:T(8,128)S(1)}) custom-call(s32[4]{0:T(128)S(1)} %pad_add_fusion.place_ref.refs_0_, f32[128,4096]{1,0:T(8,128)S(1)} %bitcast.15), custom_call_target="tpu_custom_call" | custom-call | flops 3000000000 | bytes 4000000 | tf_op jit(solution)/shard_map/pallas_call | solution.py:205
  26.0 0.0 copy-start
  26.0 0.0 copy-start.1
  26.0 0.0 copy-start.3
  26.0 0.0 copy-start.4
  26.1 0.0 collective-permute-done
  26.1 0.1 collective-permute-start.1
  26.2 0.1 broadcast_in_dim.4
  26.2 27.1 %all_to_all.10.refs_1_ = f32[32,2,16,128]{3,2,1,0:T(8,128)S(1)} all-to-all(f32[32,2,16,128]{3,2,1,0:T(8,128)S(1)} %broadcast_in_dim.4), channel_id=1, replica_groups={{0,8,22,30,36,44,50,58,64,72,86,94,100,108,114,122,132,140,146,154,160,..., dimensions={0} | all-to-all | bytes 1048576 | tf_op jit(solution)/shard_map/all_to_all | solution.py:532
  53.3 0.9 %collective-permute-start.2 = (f32[16,2,16,128]{3,2,1,0:T(8,128)S(1)}, f32[16,2,16,128]{3,2,1,0:T(8,128)S(1)}, u32[]{:S(2)}, u32[]{:S(2)}) collective-permute-start(f32[16,2,16,128]{3,2,1,0:T(8,128)S(1)} %get-tuple-element.34), channel_id=1, source_target_pairs={{0,6},{2,0},{4,2},{6,4},{8,14},{10,8},{12,10},{14,12},{1,7},{3,1},... | collective-permute-start | bytes 786440 | tf_op jit(solution)/shard_map/ppermute | solution.py:543
  54.3 1.0 %collective-permute-start.3 = (f32[16,2,16,128]{3,2,1,0:T(8,128)S(1)}, f32[16,2,16,128]{3,2,1,0:T(8,128)S(1)}, u32[]{:S(2)}, u32[]{:S(2)}) collective-permute-start(f32[16,2,16,128]{3,2,1,0:T(8,128)S(1)} %get-tuple-element.33), channel_id=1, source_target_pairs={{0,112},{16,0},{32,16},{48,32},{64,48},{80,64},{96,80},{112,96},{1... | collective-permute-start | bytes 786440 | tf_op jit(solution)/shard_map/ppermute | solution.py:544
  55.3 2.6 %collective-permute-start.5 = (f32[16,2,16,128]{3,2,1,0:T(8,128)S(1)}, f32[16,2,16,128]{3,2,1,0:T(8,128)S(1)}, u32[]{:S(2)}, u32[]{:S(2)}) collective-permute-start(f32[16,2,16,128]{3,2,1,0:T(8,128)S(1)} %get-tuple-element.33), channel_id=1, source_target_pairs={{0,136},{2,138},{4,140},{6,142},{128,0},{130,2},{132,4},{134,6},{8... | collective-permute-start | bytes 786440 | tf_op jit(solution)/shard_map/ppermute | solution.py:546
  57.9 0.8 collective-permute-start.6
  58.7 1.5 %collective-permute-start.7 = (f32[16,2,16,128]{3,2,1,0:T(8,128)S(1)}, f32[16,2,16,128]{3,2,1,0:T(8,128)S(1)}, u32[]{:S(2)}, u32[]{:S(2)}) collective-permute-start(f32[16,2,16,128]{3,2,1,0:T(8,128)S(1)} %get-tuple-element.33), channel_id=1, source_target_pairs={{0,16},{16,32},{32,48},{48,64},{64,80},{80,96},{96,112},{112,0},{1... | collective-permute-start | bytes 786440 | tf_op jit(solution)/shard_map/ppermute | solution.py:548
  60.2 5.8 %shard_map.75.refs_8_ = f32[2,9,4,128,128]{4,3,2,1,0:T(8,128)S(1)} custom-call(s32[4]{0:T(128)S(1)} %pad_add_fusion.place_ref.refs_0_, s32[2]{0:T(128)S(1)} %copy-done.3, f32[8,3]{1,0:T(8,128)S(1)} %copy-done.4, f32[16,128,128]{2,1,0:T(8,128)S(1)} %get-tuple-element.29.mine_ref, f32[16,128,128]{2,1,0:T(8,128)S(1)} %collective-permute-done.1.other_ref, ...), custom_call_target="tpu_custom_call" | custom-call | flops 6000000000 | bytes 7000000 | tf_op jit(solution)/shard_map/pallas_call | solution.py:359
  66.1 4.7 %shard_map.76 = (f32[16,2,32,128]{3,2,1,0:T(8,128)S(1)}, f32[16,2,32,128]{3,2,1,0:T(8,128)S(1)}) custom-call(s32[4]{0:T(128)S(1)} %pad_add_fusion.place_ref.refs_0_, f32[32,2,16,128]{3,2,1,0:T(8,128)S(1)} %all_to_all.10.refs_1_, f32[16,2,16,128]{3,2,1,0:T(8,128)S(1)} %collective-permute-done.2.refs_2_, ...), custom_call_target="tpu_custom_call" | custom-call | tf_op jit(solution)/shard_map/pallas_call | solution.py:433
  70.8 3.7 %collective-permute-start.8 = (f32[16,2,32,128]{3,2,1,0:T(8,128)S(1)}, f32[16,2,32,128]{3,2,1,0:T(8,128)S(1)}, u32[]{:S(2)}, u32[]{:S(2)}) collective-permute-start(f32[16,2,32,128]{3,2,1,0:T(8,128)S(1)} %get-tuple-element.32), channel_id=1, source_target_pairs={{0,1},{1,0},{2,3},{3,2},{4,5},{5,4},{6,7},{7,6},{8,9},{9,8},{10,11... | collective-permute-start | bytes 1572872 | tf_op jit(solution)/shard_map/ppermute | solution.py:515
  74.5 1.5 %collective-permute-done.8.other_ref = f32[16,2,32,128]{3,2,1,0:T(8,128)S(1)} collective-permute-done((f32[16,2,32,128]{3,2,1,0:T(8,128)S(1)}, f32[16,2,32,128]{3,2,1,0:T(8,128)S(1)}, u32[]{:S(2)}, u32[]{:S(2)}) %collective-permute-start.8) | collective-permute-done | bytes 524320 | tf_op jit(solution)/shard_map/ppermute | solution.py:515
  76.0 2.2 %shard_map.77 = f32[2,32,4096]{2,1,0:T(8,128)} custom-call(s32[4]{0:T(128)S(1)} %pad_add_fusion.place_ref.refs_0_, f32[16,2,32,128]{3,2,1,0:T(8,128)S(1)} %get-tuple-element.31.mine_ref, f32[16,2,32,128]{3,2,1,0:T(8,128)S(1)} %collective-permute-done.8.other_ref), custom_call_target="tpu_custom_call" | custom-call | tf_op jit(solution)/shard_map/pallas_call | solution.py:469
  (17 shorter events, 0.1 us)
Async XLA Ops:
  0.0 24.3 %copy-start.2 = (f32[1,4,32,4096]{3,2,1,0:T(8,128)S(1)}, f32[1,4,32,4096]{3,2,1,0:T(8,128)}, u32[]{:S(2)}) copy-start(f32[1,4,32,4096]{3,2,1,0:T(8,128)} %param.8) | copy-start | bytes 6291460
  3.1 18.9 %all-to-all-start = ((f32[16,2,16,128]{3,2,1,0:T(8,128)}), f32[16,2,16,128]{3,2,1,0:T(8,128)S(1)}, u32[]{:S(2)}, u32[]{:S(2)}) async-start(f32[16,2,16,128]{3,2,1,0:T(8,128)} %shard_map.73), calls=%async_computation | async-start | bytes 524288 | tf_op jit(solution)/shard_map/all_to_all | solution.py:522
  21.9 4.1 %collective-permute-start = (f32[16,128]{1,0:T(8,128)S(1)}, f32[16,128]{1,0:T(8,128)S(1)}, u32[]{:S(2)}, u32[]{:S(2)}) collective-permute-start(f32[16,128]{1,0:T(8,128)S(1)} %get-tuple-element.36), channel_id=1, source_target_pairs={{0,1},{1,0},{2,3},{3,2},{4,5},{5,4},{6,7},{7,6},{8,9},{9,8},{10,11... | collective-permute-start | bytes 24584 | tf_op jit(solution)/shard_map/ppermute | solution.py:515
  26.0 34.2 %copy-start = (f32[2,256,256]{2,1,0:T(8,128)S(1)}, f32[2,256,256]{2,1,0:T(8,128)}, u32[]{:S(2)}) copy-start(f32[2,256,256]{2,1,0:T(8,128)} %constant.55.clone.lane_ref.refs_9_) | copy-start | bytes 1572868
  26.0 34.2 %copy-start.1 = (f32[128,128]{1,0:T(8,128)S(1)}, f32[128,128]{1,0:T(8,128)}, u32[]{:S(2)}) copy-start(f32[128,128]{1,0:T(8,128)} %constant.56.clone.row_ref.refs_10_) | copy-start | bytes 196612
  26.0 34.2 %copy-start.3 = (s32[2]{0:T(128)S(1)}, s32[2]{0:T(128)}, u32[]{:S(2)}) copy-start(s32[2]{0:T(128)} %turn_ref.1) | copy-start | bytes 28
  26.0 34.2 %copy-start.4 = (f32[8,3]{1,0:T(8,128)S(1)}, f32[8,3]{1,0:T(8,128)}, u32[]{:S(2)}) copy-start(f32[8,3]{1,0:T(8,128)} %constant.57.clone.signs_ref) | copy-start | bytes 292
  26.1 27.2 %collective-permute-start.1 = (f32[16,128,128]{2,1,0:T(8,128)S(1)}, f32[16,128,128]{2,1,0:T(8,128)S(1)}, u32[]{:S(2)}, u32[]{:S(2)}) collective-permute-start(f32[16,128,128]{2,1,0:T(8,128)S(1)} %get-tuple-element.27), channel_id=1, source_target_pairs={{0,1},{1,0},{2,3},{3,2},{4,5},{5,4},{6,7},{7,6},{8,9},{9,8},{10,11... | collective-permute-start | bytes 3145736 | tf_op jit(solution)/shard_map/ppermute | solution.py:515
  53.3 5.3 %collective-permute-start.2 = (f32[16,2,16,128]{3,2,1,0:T(8,128)S(1)}, f32[16,2,16,128]{3,2,1,0:T(8,128)S(1)}, u32[]{:S(2)}, u32[]{:S(2)}) collective-permute-start(f32[16,2,16,128]{3,2,1,0:T(8,128)S(1)} %get-tuple-element.34), channel_id=1, source_target_pairs={{0,6},{2,0},{4,2},{6,4},{8,14},{10,8},{12,10},{14,12},{1,7},{3,1},... | collective-permute-start | bytes 786440 | tf_op jit(solution)/shard_map/ppermute | solution.py:543
  54.3 11.8 %collective-permute-start.4 = (f32[16,2,16,128]{3,2,1,0:T(8,128)S(1)}, f32[16,2,16,128]{3,2,1,0:T(8,128)S(1)}, u32[]{:S(2)}, u32[]{:S(2)}) collective-permute-start(f32[16,2,16,128]{3,2,1,0:T(8,128)S(1)} %get-tuple-element.34), channel_id=1, source_target_pairs={{0,128},{2,130},{4,132},{6,134},{128,8},{130,10},{132,12},{134,14}... | collective-permute-start | bytes 786440 | tf_op jit(solution)/shard_map/ppermute | solution.py:545
  54.3 11.8 %collective-permute-start.3 = (f32[16,2,16,128]{3,2,1,0:T(8,128)S(1)}, f32[16,2,16,128]{3,2,1,0:T(8,128)S(1)}, u32[]{:S(2)}, u32[]{:S(2)}) collective-permute-start(f32[16,2,16,128]{3,2,1,0:T(8,128)S(1)} %get-tuple-element.33), channel_id=1, source_target_pairs={{0,112},{16,0},{32,16},{48,32},{64,48},{80,64},{96,80},{112,96},{1... | collective-permute-start | bytes 786440 | tf_op jit(solution)/shard_map/ppermute | solution.py:544
  55.3 10.7 %collective-permute-start.5 = (f32[16,2,16,128]{3,2,1,0:T(8,128)S(1)}, f32[16,2,16,128]{3,2,1,0:T(8,128)S(1)}, u32[]{:S(2)}, u32[]{:S(2)}) collective-permute-start(f32[16,2,16,128]{3,2,1,0:T(8,128)S(1)} %get-tuple-element.33), channel_id=1, source_target_pairs={{0,136},{2,138},{4,140},{6,142},{128,0},{130,2},{132,4},{134,6},{8... | collective-permute-start | bytes 786440 | tf_op jit(solution)/shard_map/ppermute | solution.py:546
  57.9 8.2 %collective-permute-start.6 = (f32[16,2,16,128]{3,2,1,0:T(8,128)S(1)}, f32[16,2,16,128]{3,2,1,0:T(8,128)S(1)}, u32[]{:S(2)}, u32[]{:S(2)}) collective-permute-start(f32[16,2,16,128]{3,2,1,0:T(8,128)S(1)} %get-tuple-element.34), channel_id=1, source_target_pairs={{0,2},{2,4},{4,6},{6,0},{8,10},{10,12},{12,14},{14,8},{1,3},{3,5},... | collective-permute-start | bytes 786440 | tf_op jit(solution)/shard_map/ppermute | solution.py:547
  58.7 7.4 %collective-permute-start.7 = (f32[16,2,16,128]{3,2,1,0:T(8,128)S(1)}, f32[16,2,16,128]{3,2,1,0:T(8,128)S(1)}, u32[]{:S(2)}, u32[]{:S(2)}) collective-permute-start(f32[16,2,16,128]{3,2,1,0:T(8,128)S(1)} %get-tuple-element.33), channel_id=1, source_target_pairs={{0,16},{16,32},{32,48},{48,64},{64,80},{80,96},{96,112},{112,0},{1... | collective-permute-start | bytes 786440 | tf_op jit(solution)/shard_map/ppermute | solution.py:548
  70.8 5.2 %collective-permute-start.8 = (f32[16,2,32,128]{3,2,1,0:T(8,128)S(1)}, f32[16,2,32,128]{3,2,1,0:T(8,128)S(1)}, u32[]{:S(2)}, u32[]{:S(2)}) collective-permute-start(f32[16,2,32,128]{3,2,1,0:T(8,128)S(1)} %get-tuple-element.32), channel_id=1, source_target_pairs={{0,1},{1,0},{2,3},{3,2},{4,5},{5,4},{6,7},{7,6},{8,9},{9,8},{10,11... | collective-permute-start | bytes 1572872 | tf_op jit(solution)/shard_map/ppermute | solution.py:515

commit v3 on v2

--- a/solution.py
+++ b/solution.py
@@ -16,18 +16,6 @@
 COLORS = 4
 
 
-ROTATIONS = [
-    (False, 1, 1, 1),
-    (True, -1, 1, 1),
-    (False, -1, 1, -1),
-    (True, 1, 1, -1),
-    (False, -1, -1, 1),
-    (True, 1, -1, 1),
-    (False, 1, -1, -1),
-    (True, -1, -1, -1),
-]
-
-
 def dft(n):
     phase = np.outer(np.arange(n), np.arange(n)) % n * (2 * math.pi / n)
     return np.cos(phase), np.sin(phase)
@@ -42,7 +30,10 @@
     return np.stack([plain, turned]).astype(np.float32), rows.astype(np.float32)
 
 
-SIGNS = np.array([[signs[1], signs[2], signs[3]] for signs in ROTATIONS], np.float32)
+def signs_of(turn):
+    quarter, mirror = lax.rem(turn, 4), jnp.where(turn >= 4, -1.0, 1.0)
+    row = jnp.where(jnp.logical_or(quarter == 1, quarter == 2), -1.0, 1.0)
+    return row * mirror, mirror, jnp.where(quarter >= 2, -1.0, 1.0)
 
 
 def split(value):
@@ -173,7 +164,8 @@
     return real_inverse(spectrum)
 
 
-def forward_y_kernel(place_ref, grid_ref, mine_ref, other_ref):
+def forward_y_kernel(grid_ref, mine_ref, other_ref):
+    core = lax.axis_index("slab")
     count = grid_ref.shape[1] // 128
     rows = mine_ref.shape[1]
 
@@ -190,26 +182,26 @@
 
         lax.fori_loop(0, rows // 8, step, 0, unroll=UNROLL)
 
-    @pl.when(place_ref[0] == 0)
+    @pl.when(core == 0)
     def _():
         run(mine_ref, other_ref)
 
-    @pl.when(place_ref[0] == 1)
+    @pl.when(core == 1)
     def _():
         run(other_ref, mine_ref)
 
 
-def forward_y(place, grid):
+def forward_y(grid):
     rows, width = grid.shape
     out = jax.ShapeDtypeStruct((width // 256, rows, 128), F32)
     return pl.pallas_call(
         forward_y_kernel,
-        in_specs=[SMEM, VMEM],
+        in_specs=[VMEM],
         out_specs=[VMEM, VMEM],
         out_shape=[out, out],
         cost_estimate=pl.CostEstimate(flops=3 * 10**9, bytes_accessed=4 * 10**6, transcendentals=0),
         compiler_params=pltpu.CompilerParams(vmem_limit_bytes=40 * 1024 * 1024),
-    )(place, grid)
+    )(grid)
 
 
 RING_X, RING_Y, RING_Z = 4, 4, 8
@@ -260,14 +252,13 @@
 
 
 def unit_tiles(step, odd, first_re, first_im):
+    if step == 0:
+        return first_re, first_im * odd
+    if step < STEPS - 1:
+        return first_re, first_im
     left = lax.broadcasted_iota(jnp.int32, first_re.shape, 1) < first_re.shape[1] // 2
     mask = jnp.where(left, 1.0 - odd, 0.0)
-    rolled = pltpu.roll(first_im, first_im.shape[1] // 2, 1)
-    keep = jnp.where(step == 0, odd, 1.0)
-    extra = step == STEPS - 1
-    re = jnp.where(extra, first_im * mask, first_re)
-    im = jnp.where(extra, rolled * mask, first_im * keep)
-    return re, im
+    return first_im * mask, pltpu.roll(first_im, first_im.shape[1] // 2, 1) * mask
 
 
 def signed(table, rows, cols, down, right, both):
@@ -278,6 +269,7 @@
 
 STEPS = 9
 BATCH = 9
+PRODUCT_BATCH = 9
 
 
 def rows_of(lanes):
@@ -297,15 +289,15 @@
     )
 
 
-def spectrum_kernel(place_ref, turn_ref, signs_ref, mine_ref, other_ref, lane_ref, row_ref, out_ref, lane_work):
-    place = place_ref[0]
+def spectrum_kernel(turn_ref, mine_ref, other_ref, lane_ref, row_ref, out_ref, lane_work):
+    place = lax.axis_index("slab")
     odd = place.astype(F32)
     channels = mine_ref.shape[1] // 32
     slots = out_ref.shape[0]
     is_low = place == 0
 
     def tiles(step, c):
-        unit = lax.rem(step, STEPS - 1)
+        unit = step % (STEPS - 1)
         at = pl.ds(c * 32, 32)
         parts = []
         for part in range(2):
@@ -317,7 +309,7 @@
 
     for slot in range(slots):
         turn = turn_ref[slot]
-        sx, sy, sz = (signs_ref[turn, k] for k in range(3))
+        sx, sy, sz = signs_of(turn)
         row_table = row_stack(signed(row_ref[...], 64, 64, sx, sx, 1.0))
 
         def run(swapped):
@@ -341,7 +333,8 @@
                         out_ref[slot, count * BATCH + d, c] = done[:, at : at + 128]
                 return carry
 
-            lax.fori_loop(0, STEPS // BATCH, step, 0)
+            for count in range(STEPS // BATCH):
+                step(count, 0)
 
         @pl.when(lax.rem(turn, 2) == 0)
         def _():
@@ -352,28 +345,29 @@
             run(True)
 
 
-def spectrum(place, turns, signs, mine, other, lane, row):
+def spectrum(turns, mine, other, lane, row):
     pieces, rows, _ = mine.shape
     slots = turns.shape[0]
     channels = rows // 32
     return pl.pallas_call(
         spectrum_kernel,
-        in_specs=[SMEM, SMEM, SMEM, VMEM, VMEM, VMEM, VMEM],
+        in_specs=[SMEM, VMEM, VMEM, VMEM, VMEM],
         out_specs=VMEM,
         scratch_shapes=[pltpu.VMEM((768, 256), BF16)],
         out_shape=jax.ShapeDtypeStruct((slots, STEPS, channels, 128, 128), F32),
         cost_estimate=pl.CostEstimate(flops=6 * 10**9, bytes_accessed=7 * 10**6, transcendentals=0),
         compiler_params=pltpu.CompilerParams(vmem_limit_bytes=40 * 1024 * 1024),
-    )(place, turns, signs, mine, other, lane, row)
+    )(turns, mine, other, lane, row)
 
 
 def product_kernel(
-    factor, place_ref, own_ref, up_a, up_b, far_a, far_b, down_a, down_b, lig_ref, lane_ref, row_ref,
+    factor, own_ref, up_a, up_b, far_a, far_b, down_a, down_b, lig_ref, lane_ref, row_ref,
     mine_ref, other_ref, lane_work, back_work, planes,
 ):
-    place = place_ref[0]
+    place = lax.axis_index("slab")
     odd = place.astype(F32)
     slots, steps, channels = lig_ref.shape[:3]
+    tone = color(lax.axis_index("lig") % RING_X, lax.axis_index("yl"), lax.axis_index("z"))
     lane_work[...] = lane_stack(lane_ref[0])
     back_work[...] = lane_stack(signed(lane_ref[0] * factor, 128, 128, -1.0, -1.0, 1.0))
     row_table = row_stack(row_ref[...])
@@ -390,49 +384,53 @@
             ref, at = rest[turn - 1][piece // half], 2 * (piece % half)
         return jnp.concatenate([ref[at + p, s ^ place] for s in range(2) for p in range(2)], axis=0)
 
-    grids = []
-    for u in range(steps):
-        unit = u % (steps - 1)
-        for turn in range(channels):
-            re, im = unit_tiles(u, odd, tile(turn, 2 * unit), tile(turn, 2 * unit + 1))
-            grids.append(jnp.concatenate([re, im], axis=1))
-    along = lane_dot(jnp.concatenate(grids, axis=0), lane_work[...])
-    rec = row_dot(row_table, rows_of(along))
-    sums = []
-    for u in range(steps):
-        for i in range(slots):
+    left = lax.broadcasted_iota(jnp.int32, (slots * 64, 128), 1) < 64
+    extra = None
+    order = [steps - 1, *range(steps - 1)]
+    for group in (order[at : at + PRODUCT_BATCH] for at in range(0, steps, PRODUCT_BATCH)):
+        grids = []
+        for u in group:
+            unit = u % (steps - 1)
             for turn in range(channels):
-                c = lax.rem(place_ref[3] + turn, channels)
-                at = (u * channels + turn) * 128
-                rec_re, rec_im = rec[:64, at : at + 128], rec[64:, at : at + 128]
-                re, im = lig_ref[i, u, c, :64], lig_ref[i, u, c, 64:]
-                term = (rec_re * re + rec_im * im, rec_re * im - rec_im * re)
-                total = term if turn == 0 else (total[0] + term[0], total[1] + term[1])
-            sums.append(jnp.concatenate(total, axis=0))
-    rows = row_dot(back_row, jnp.concatenate(sums, axis=1))
-    back = lane_dot(lanes_of(rows), back_work[...])
-    parts = [back[u * slots * 64 : (u + 1) * slots * 64] for u in range(steps)]
-    re, im = parts[-1][:, :128], parts[-1][:, 128:]
-    left = lax.broadcasted_iota(jnp.int32, re.shape, 1) < 64
-    extra = jnp.where(left, re, pltpu.roll(im, 64, 1))
-    for u in range(steps - 1):
-        re, im = parts[u][:, :128], parts[u][:, 128:]
-        if u == 0:
-            im = jnp.where(place == 0, extra, im)
-        for part, value in enumerate((re, im)):
-            planes[2 * u + part] = value.reshape(slots, 64, 128)
+                re, im = unit_tiles(u, odd, tile(turn, 2 * unit), tile(turn, 2 * unit + 1))
+                grids.append(jnp.concatenate([re, im], axis=1))
+        along = lane_dot(jnp.concatenate(grids, axis=0), lane_work[...])
+        rec = row_dot(row_table, rows_of(along))
+        sums = []
+        for d, u in enumerate(group):
             for i in range(slots):
-                mine_ref[2 * u + part, i] = planes[2 * u + part, i, own, :]
-                other_ref[2 * u + part, i] = planes[2 * u + part, i, far, :]
-
-
-def product(place, rec, lig, lane, row, factor):
+                for turn in range(channels):
+                    c = lax.rem(tone + turn, channels)
+                    at = (d * channels + turn) * 128
+                    rec_re, rec_im = rec[:64, at : at + 128], rec[64:, at : at + 128]
+                    re, im = lig_ref[i, u, c, :64], lig_ref[i, u, c, 64:]
+                    term = (rec_re * re + rec_im * im, rec_re * im - rec_im * re)
+                    total = term if turn == 0 else (total[0] + term[0], total[1] + term[1])
+                sums.append(jnp.concatenate(total, axis=0))
+        rows = row_dot(back_row, jnp.concatenate(sums, axis=1))
+        back = lane_dot(lanes_of(rows), back_work[...])
+        for d, u in enumerate(group):
+            part = back[d * slots * 64 : (d + 1) * slots * 64]
+            re, im = part[:, :128], part[:, 128:]
+            if u == steps - 1:
+                extra = jnp.where(left, re, pltpu.roll(im, 64, 1))
+                continue
+            if u == 0:
+                im = jnp.where(place == 0, extra, im)
+            for half, value in enumerate((re, im)):
+                planes[2 * u + half] = value.reshape(slots, 64, 128)
+                for i in range(slots):
+                    mine_ref[2 * u + half, i] = planes[2 * u + half, i, own, :]
+                    other_ref[2 * u + half, i] = planes[2 * u + half, i, far, :]
+
+
+def product(rec, lig, lane, row, factor):
     slots = lig.shape[0]
     pieces = 2 * (lig.shape[1] - 1)
     out = jax.ShapeDtypeStruct((pieces, slots, 32, 128), F32)
     return pl.pallas_call(
         lambda *refs: product_kernel(factor, *refs),
-        in_specs=[SMEM] + [VMEM] * (len(rec) + 3),
+        in_specs=[VMEM] * (len(rec) + 3),
         out_specs=[VMEM, VMEM],
         scratch_shapes=[
             pltpu.VMEM((768, 256), BF16),
@@ -441,16 +439,16 @@
         ],
         out_shape=[out, out],
         compiler_params=pltpu.CompilerParams(vmem_limit_bytes=40 * 1024 * 1024),
-    )(place, *rec, lig, lane, row)
-
-
-def inverse_y_kernel(place_ref, mine_ref, other_ref, out_ref):
-    pieces, slots, rows, _ = mine_ref.shape
-    is_low = place_ref[0] == 0
+    )(*rec, lig, lane, row)
+
+
+def inverse_y_kernel(mine_ref, other_ref, out_ref):
+    pieces, _, rows, _ = mine_ref.shape
+    is_low = lax.axis_index("slab") == 0
+    slot = pl.program_id(0)
 
     def step(tile, carry):
-        slot = tile // (rows // 8)
-        at = pl.ds(pl.multiple_of(tile % (rows // 8) * 8, 8), 8)
+        at = pl.ds(pl.multiple_of(tile * 8, 8), 8)
         low, high = [], []
         for k in range(pieces // 2):
             own = [mine_ref[2 * k + part, slot, at, :] for part in range(2)]
@@ -458,21 +456,22 @@
             low.append(tuple(jnp.where(is_low, a, b) for a, b in zip(own, far)))
             high.append(tuple(jnp.where(is_low, b, a) for a, b in zip(own, far)))
         for b, value in enumerate(y_inverse(low + high)):
-            out_ref[slot, at, b * 128 : (b + 1) * 128] = value
+            out_ref[0, at, b * 128 : (b + 1) * 128] = value
         return carry
 
-    lax.fori_loop(0, slots * (rows // 8), step, 0, unroll=UNROLL)
-
-
-def inverse_y(place, mine, other):
+    lax.fori_loop(0, rows // 8, step, 0, unroll=UNROLL)
+
+
+def inverse_y(mine, other):
     pieces, slots, rows, _ = mine.shape
     return pl.pallas_call(
         inverse_y_kernel,
-        in_specs=[SMEM, VMEM, VMEM],
-        out_specs=VMEM,
+        grid=(slots,),
+        in_specs=[VMEM, VMEM],
+        out_specs=pl.BlockSpec((1, rows, pieces * 256), lambda i: (i, 0, 0)),
         out_shape=jax.ShapeDtypeStruct((slots, rows, pieces * 256), F32),
         compiler_params=pltpu.CompilerParams(vmem_limit_bytes=40 * 1024 * 1024),
-    )(place, mine, other)
+    )(mine, other)
 
 
 def color(x, y, z):
@@ -508,22 +507,16 @@
 def per_device(receptors, ligands, plan, rotations):
     _, channels, half, flat = ligands.shape
     length = 2 * half
-    core = lax.axis_index("slab")
-    y_hi, x = lax.axis_index("lig") // RING_X, lax.axis_index("lig") % RING_X
-    tone = color(x, lax.axis_index("yl"), lax.axis_index("z"))
-    place = jnp.stack([core, x, y_hi, tone]).astype(jnp.int32)
     swap = lambda value: lax.ppermute(value, "slab", [(0, 1), (1, 0)])
     lane, row = (jnp.asarray(table) for table in base_tables(length))
-    signs = jnp.asarray(SIGNS)
     factor = 1.0 / (math.sqrt(channels * length**3) * length**3)
 
     rec_share = forward_rec(receptors.reshape(channels * half, flat))
-    rec_share, root = lax.optimization_barrier((rec_share, plan[0].astype(jnp.uint32)))
     scattered = lax.all_to_all(rec_share, ("yl", "z"), split_axis=0, concat_axis=0)
     scattered, ligands = lax.optimization_barrier((scattered, ligands))
-    piece = lax.dynamic_index_in_dim(scattered, root, 0, False)
+    piece = lax.dynamic_index_in_dim(scattered, plan[0], 0, False)
     piece_far = swap(piece[1])
-    lig_mine, lig_other = forward_y(place, ligands.reshape(channels * half, flat))
+    lig_mine, lig_other = forward_y(ligands.reshape(channels * half, flat))
     piece_far, lig_mine, lig_other = lax.optimization_barrier((piece_far, lig_mine, lig_other))
     lig_far = swap(lig_other)
     piece = jnp.stack([piece[0], piece_far])[None]
@@ -547,11 +540,11 @@
         lax.ppermute(first, "lig", shift_x(1)),
         lax.ppermute(second, "z", shift_z(1)),
     ]
-    lig_spec = spectrum(place, rotations, signs, lig_mine, lig_far, lane, row)
-
-    out_mine, out_other = product(place, rec, lig_spec, lane, row, factor)
+    lig_spec = spectrum(rotations, lig_mine, lig_far, lane, row)
+
+    out_mine, out_other = product(rec, lig_spec, lane, row, factor)
     out_far = swap(out_other)
-    scores = inverse_y(place, out_mine, out_far)
+    scores = inverse_y(out_mine, out_far)
     return scores[None, :, None]
 
 

time: 78.4 us -> 75.9 us (0.968)
  Pallas kernels: 16.8 us -> 15 us
    pallas_call x4, Pallas kernels: 14.4 us -> 12.6 us  [the longest x1 5.83 us: spectrum(): pl.pallas_call(spectrum_kernel, in_specs=[SMEM, VMEM, VMEM, VMEM, VMEM],...]
  transfers between devices with their start and end apart: 10 -> 10, of which waited for: 2 -> 2; matrix products, arithmetic and copies ran while one was open for 0% -> 0% of each run, Pallas kernels for 10% -> 9%
where the time goes in v3:
time: 75.9 us; the launch traced here: 75.7 us
  blocking collectives  27.1 us (36%)
  starting transfers between devices  23.1 us (30%)
  Pallas kernels  15 us (20%)
  waiting for transfers between devices  9.64 us (13%)
  between operations  0.78 us (1%)
    all_to_all x1, blocking collectives, per_device(): lax.all_to_all(jnp.broadcast_to(piece, (len(groups[0]), *piece.shape[1:])...  27.1 us
    all_to_all x1, starting transfers between devices, per_device(): lax.all_to_all(rec_share, ('yl', 'z'), split_axis=0, concat_axis=0)  10.1 us
    all_to_all x1, waiting for transfers between devices, per_device(): lax.all_to_all(rec_share, ('yl', 'z'), split_axis=0, concat_axis=0)  8.08 us
    ppermute x3, starting transfers between devices, per_device(): swap = lambda value: lax.ppermute(value, 'slab', [(0, 1), (1, 0)])  6.12 us
    pallas_call x1, Pallas kernels, spectrum(): pl.pallas_call(spectrum_kernel, in_specs=[SMEM, VMEM, VMEM, VMEM, VMEM],...  5.83 us
    pallas_call x1, Pallas kernels, product(): pl.pallas_call(lambda *refs: product_kernel(factor, *refs), in_specs=[VME...  4.15 us
    ppermute x1, starting transfers between devices, per_device(): lax.ppermute(second, ('yl', 'lig'), shift_y(-1))  2.57 us
    pallas_call x1, Pallas kernels, forward_rec(): pl.pallas_call(forward_rec_kernel, in_specs=[pl.BlockSpec(memory_space=pl...  2.41 us
  transfers between devices with their start and end apart: 10, of which 2 were waited for; matrix products, arithmetic and copies ran while one was open for 0% of the time, Pallas kernels for 9%

profile of v3, /device:TPU:1, one launch (start us, length us, event | category | flops | bytes accessed | tf_op | source)
XLA Modules:
  0.0 75.7 jit_solution(8844235607603350608)
XLA Ops:
  0.0 2.4 %shard_map.64 = f32[16,2,16,128]{3,2,1,0:T(8,128)} custom-call(f32[128,4096]{1,0:T(8,128)} %bitcast.15), custom_call_target="tpu_custom_call" | custom-call | tf_op jit(solution)/shard_map/pallas_call | solution.py:241
  2.4 10.1 %all-to-all-start = ((f32[16,2,16,128]{3,2,1,0:T(8,128)}), f32[16,2,16,128]{3,2,1,0:T(8,128)S(1)}, u32[]{:S(2)}, u32[]{:S(2)}) async-start(f32[16,2,16,128]{3,2,1,0:T(8,128)} %shard_map.64), calls=%async_computation | async-start | bytes 524288 | tf_op jit(solution)/shard_map/all_to_all | solution.py:515
  13.2 8.1 %all-to-all-done = f32[16,2,16,128]{3,2,1,0:T(8,128)S(1)} async-done(((f32[16,2,16,128]{3,2,1,0:T(8,128)}), f32[16,2,16,128]{3,2,1,0:T(8,128)S(1)}, u32[]{:S(2)}, u32[]{:S(2)}) %all-to-all-start) | async-done | bytes 262176 | tf_op jit(solution)/shard_map/all_to_all | solution.py:515
  21.3 2.3 %collective-permute-start = (f32[16,128]{1,0:T(8,128)S(1)}, f32[16,128]{1,0:T(8,128)S(1)}, u32[]{:S(2)}, u32[]{:S(2)}) collective-permute-start(f32[16,128]{1,0:T(8,128)S(1)} %get-tuple-element.32), channel_id=1, source_target_pairs={{0,1},{1,0},{2,3},{3,2},{4,5},{5,4},{6,7},{7,6},{8,9},{9,8},{10,11... | collective-permute-start | bytes 24584 | tf_op jit(solution)/shard_map/ppermute | solution.py:510
  23.6 1.1 %shard_map.65 = (f32[16,128,128]{2,1,0:T(8,128)S(1)}, f32[16,128,128]{2,1,0:T(8,128)S(1)}) custom-call(f32[128,4096]{1,0:T(8,128)S(1)} %bitcast.14), custom_call_target="tpu_custom_call" | custom-call | flops 3000000000 | bytes 4000000 | tf_op jit(solution)/shard_map/pallas_call | solution.py:197
  24.8 0.0 copy-start
  24.8 0.0 copy-start.1
  24.8 0.0 copy-start.3
  24.8 0.0 collective-permute-done
  24.9 0.1 collective-permute-start.1
  25.0 0.1 broadcast_in_dim.4
  25.0 27.1 %all_to_all.10.refs_0_ = f32[32,2,16,128]{3,2,1,0:T(8,128)S(1)} all-to-all(f32[32,2,16,128]{3,2,1,0:T(8,128)S(1)} %broadcast_in_dim.4), channel_id=1, replica_groups={{0,8,22,30,36,44,50,58,64,72,86,94,100,108,114,122,132,140,146,154,160,..., dimensions={0} | all-to-all | bytes 1048576 | tf_op jit(solution)/shard_map/all_to_all | solution.py:525
  52.1 0.0 collective-permute-done.1.other_ref
  52.1 0.9 %collective-permute-start.2 = (f32[16,2,16,128]{3,2,1,0:T(8,128)S(1)}, f32[16,2,16,128]{3,2,1,0:T(8,128)S(1)}, u32[]{:S(2)}, u32[]{:S(2)}) collective-permute-start(f32[16,2,16,128]{3,2,1,0:T(8,128)S(1)} %get-tuple-element.30), channel_id=1, source_target_pairs={{0,6},{2,0},{4,2},{6,4},{8,14},{10,8},{12,10},{14,12},{1,7},{3,1},... | collective-permute-start | bytes 786440 | tf_op jit(solution)/shard_map/ppermute | solution.py:536
  53.1 0.0 collective-permute-start.4
  53.1 1.0 %collective-permute-start.3 = (f32[16,2,16,128]{3,2,1,0:T(8,128)S(1)}, f32[16,2,16,128]{3,2,1,0:T(8,128)S(1)}, u32[]{:S(2)}, u32[]{:S(2)}) collective-permute-start(f32[16,2,16,128]{3,2,1,0:T(8,128)S(1)} %get-tuple-element.29), channel_id=1, source_target_pairs={{0,112},{16,0},{32,16},{48,32},{64,48},{80,64},{96,80},{112,96},{1... | collective-permute-start | bytes 786440 | tf_op jit(solution)/shard_map/ppermute | solution.py:537
  54.1 2.6 %collective-permute-start.5 = (f32[16,2,16,128]{3,2,1,0:T(8,128)S(1)}, f32[16,2,16,128]{3,2,1,0:T(8,128)S(1)}, u32[]{:S(2)}, u32[]{:S(2)}) collective-permute-start(f32[16,2,16,128]{3,2,1,0:T(8,128)S(1)} %get-tuple-element.29), channel_id=1, source_target_pairs={{0,136},{2,138},{4,140},{6,142},{128,0},{130,2},{132,4},{134,6},{8... | collective-permute-start | bytes 786440 | tf_op jit(solution)/shard_map/ppermute | solution.py:539
  56.7 0.8 %collective-permute-start.6 = (f32[16,2,16,128]{3,2,1,0:T(8,128)S(1)}, f32[16,2,16,128]{3,2,1,0:T(8,128)S(1)}, u32[]{:S(2)}, u32[]{:S(2)}) collective-permute-start(f32[16,2,16,128]{3,2,1,0:T(8,128)S(1)} %get-tuple-element.30), channel_id=1, source_target_pairs={{0,2},{2,4},{4,6},{6,0},{8,10},{10,12},{12,14},{14,8},{1,3},{3,5},... | collective-permute-start | bytes 786440 | tf_op jit(solution)/shard_map/ppermute | solution.py:540
  57.5 1.5 %collective-permute-start.7 = (f32[16,2,16,128]{3,2,1,0:T(8,128)S(1)}, f32[16,2,16,128]{3,2,1,0:T(8,128)S(1)}, u32[]{:S(2)}, u32[]{:S(2)}) collective-permute-start(f32[16,2,16,128]{3,2,1,0:T(8,128)S(1)} %get-tuple-element.29), channel_id=1, source_target_pairs={{0,16},{16,32},{32,48},{48,64},{64,80},{80,96},{96,112},{112,0},{1... | collective-permute-start | bytes 786440 | tf_op jit(solution)/shard_map/ppermute | solution.py:541
  59.0 5.8 %shard_map.66.refs_7_ = f32[2,9,4,128,128]{4,3,2,1,0:T(8,128)S(1)} custom-call(s32[2]{0:T(128)S(1)} %copy-done.3, f32[16,128,128]{2,1,0:T(8,128)S(1)} %get-tuple-element.25.mine_ref, f32[16,128,128]{2,1,0:T(8,128)S(1)} %collective-permute-done.1.other_ref, f32[2,256,256]{2,1,0:T(8,128)S(1)} %copy-done, f32[128,128]{1,0:T(8,128)S(1)} %copy-done.1), custom_call_target="tpu_custom_call" | custom-call | flops 6000000000 | bytes 7000000 | tf_op jit(solution)/shard_map/pallas_call | solution.py:352
  64.9 4.2 %shard_map.67 = (f32[16,2,32,128]{3,2,1,0:T(8,128)S(1)}, f32[16,2,32,128]{3,2,1,0:T(8,128)S(1)}) custom-call(f32[32,2,16,128]{3,2,1,0:T(8,128)S(1)} %all_to_all.10.refs_0_, f32[16,2,16,128]{3,2,1,0:T(8,128)S(1)} %collective-permute-done.2.refs_1_, f32[16,2,16,128]{3,2,1,0:T(8,128)S(1)} %collective-permute-done.3.refs_2_, ...), custom_call_target="tpu_custom_call" | custom-call | tf_op jit(solution)/shard_map/pallas_call | solution.py:431
  69.0 3.7 %collective-permute-start.8 = (f32[16,2,32,128]{3,2,1,0:T(8,128)S(1)}, f32[16,2,32,128]{3,2,1,0:T(8,128)S(1)}, u32[]{:S(2)}, u32[]{:S(2)}) collective-permute-start(f32[16,2,32,128]{3,2,1,0:T(8,128)S(1)} %get-tuple-element.28), channel_id=1, source_target_pairs={{0,1},{1,0},{2,3},{3,2},{4,5},{5,4},{6,7},{7,6},{8,9},{9,8},{10,11... | collective-permute-start | bytes 1572872 | tf_op jit(solution)/shard_map/ppermute | solution.py:510
  72.7 1.5 %collective-permute-done.8.other_ref = f32[16,2,32,128]{3,2,1,0:T(8,128)S(1)} collective-permute-done((f32[16,2,32,128]{3,2,1,0:T(8,128)S(1)}, f32[16,2,32,128]{3,2,1,0:T(8,128)S(1)}, u32[]{:S(2)}, u32[]{:S(2)}) %collective-permute-start.8) | collective-permute-done | bytes 524320 | tf_op jit(solution)/shard_map/ppermute | solution.py:510
  74.3 1.4 %shard_map.68 = f32[2,32,4096]{2,1,0:T(8,128)} custom-call(f32[16,2,32,128]{3,2,1,0:T(8,128)S(1)} %get-tuple-element.27.mine_ref, f32[16,2,32,128]{3,2,1,0:T(8,128)S(1)} %collective-permute-done.8.other_ref), custom_call_target="tpu_custom_call" | custom-call | tf_op jit(solution)/shard_map/pallas_call | solution.py:467
  (14 shorter events, 0.1 us)
Async XLA Ops:
  0.0 23.6 %copy-start.2 = (f32[1,4,32,4096]{3,2,1,0:T(8,128)S(1)}, f32[1,4,32,4096]{3,2,1,0:T(8,128)}, u32[]{:S(2)}) copy-start(f32[1,4,32,4096]{3,2,1,0:T(8,128)} %param.7) | copy-start | bytes 6291460
  2.4 18.9 %all-to-all-start = ((f32[16,2,16,128]{3,2,1,0:T(8,128)}), f32[16,2,16,128]{3,2,1,0:T(8,128)S(1)}, u32[]{:S(2)}, u32[]{:S(2)}) async-start(f32[16,2,16,128]{3,2,1,0:T(8,128)} %shard_map.64), calls=%async_computation | async-start | bytes 524288 | tf_op jit(solution)/shard_map/all_to_all | solution.py:515
  21.3 3.5 %collective-permute-start = (f32[16,128]{1,0:T(8,128)S(1)}, f32[16,128]{1,0:T(8,128)S(1)}, u32[]{:S(2)}, u32[]{:S(2)}) collective-permute-start(f32[16,128]{1,0:T(8,128)S(1)} %get-tuple-element.32), channel_id=1, source_target_pairs={{0,1},{1,0},{2,3},{3,2},{4,5},{5,4},{6,7},{7,6},{8,9},{9,8},{10,11... | collective-permute-start | bytes 24584 | tf_op jit(solution)/shard_map/ppermute | solution.py:510
  24.8 34.2 %copy-start = (f32[2,256,256]{2,1,0:T(8,128)S(1)}, f32[2,256,256]{2,1,0:T(8,128)}, u32[]{:S(2)}) copy-start(f32[2,256,256]{2,1,0:T(8,128)} %constant.10.clone.lane_ref.refs_8_) | copy-start | bytes 1572868
  24.8 34.2 %copy-start.1 = (f32[128,128]{1,0:T(8,128)S(1)}, f32[128,128]{1,0:T(8,128)}, u32[]{:S(2)}) copy-start(f32[128,128]{1,0:T(8,128)} %constant.11.clone.row_ref.refs_9_) | copy-start | bytes 196612
  24.8 34.2 %copy-start.3 = (s32[2]{0:T(128)S(1)}, s32[2]{0:T(128)}, u32[]{:S(2)}) copy-start(s32[2]{0:T(128)} %turn_ref.1) | copy-start | bytes 28
  24.9 27.2 %collective-permute-start.1 = (f32[16,128,128]{2,1,0:T(8,128)S(1)}, f32[16,128,128]{2,1,0:T(8,128)S(1)}, u32[]{:S(2)}, u32[]{:S(2)}) collective-permute-start(f32[16,128,128]{2,1,0:T(8,128)S(1)} %get-tuple-element.23), channel_id=1, source_target_pairs={{0,1},{1,0},{2,3},{3,2},{4,5},{5,4},{6,7},{7,6},{8,9},{9,8},{10,11... | collective-permute-start | bytes 3145736 | tf_op jit(solution)/shard_map/ppermute | solution.py:510
  52.1 5.4 %collective-permute-start.2 = (f32[16,2,16,128]{3,2,1,0:T(8,128)S(1)}, f32[16,2,16,128]{3,2,1,0:T(8,128)S(1)}, u32[]{:S(2)}, u32[]{:S(2)}) collective-permute-start(f32[16,2,16,128]{3,2,1,0:T(8,128)S(1)} %get-tuple-element.30), channel_id=1, source_target_pairs={{0,6},{2,0},{4,2},{6,4},{8,14},{10,8},{12,10},{14,12},{1,7},{3,1},... | collective-permute-start | bytes 786440 | tf_op jit(solution)/shard_map/ppermute | solution.py:536
  53.1 11.8 %collective-permute-start.4 = (f32[16,2,16,128]{3,2,1,0:T(8,128)S(1)}, f32[16,2,16,128]{3,2,1,0:T(8,128)S(1)}, u32[]{:S(2)}, u32[]{:S(2)}) collective-permute-start(f32[16,2,16,128]{3,2,1,0:T(8,128)S(1)} %get-tuple-element.30), channel_id=1, source_target_pairs={{0,128},{2,130},{4,132},{6,134},{128,8},{130,10},{132,12},{134,14}... | collective-permute-start | bytes 786440 | tf_op jit(solution)/shard_map/ppermute | solution.py:538
  53.1 11.8 %collective-permute-start.3 = (f32[16,2,16,128]{3,2,1,0:T(8,128)S(1)}, f32[16,2,16,128]{3,2,1,0:T(8,128)S(1)}, u32[]{:S(2)}, u32[]{:S(2)}) collective-permute-start(f32[16,2,16,128]{3,2,1,0:T(8,128)S(1)} %get-tuple-element.29), channel_id=1, source_target_pairs={{0,112},{16,0},{32,16},{48,32},{64,48},{80,64},{96,80},{112,96},{1... | collective-permute-start | bytes 786440 | tf_op jit(solution)/shard_map/ppermute | solution.py:537
  54.1 10.7 %collective-permute-start.5 = (f32[16,2,16,128]{3,2,1,0:T(8,128)S(1)}, f32[16,2,16,128]{3,2,1,0:T(8,128)S(1)}, u32[]{:S(2)}, u32[]{:S(2)}) collective-permute-start(f32[16,2,16,128]{3,2,1,0:T(8,128)S(1)} %get-tuple-element.29), channel_id=1, source_target_pairs={{0,136},{2,138},{4,140},{6,142},{128,0},{130,2},{132,4},{134,6},{8... | collective-permute-start | bytes 786440 | tf_op jit(solution)/shard_map/ppermute | solution.py:539
  56.7 8.2 %collective-permute-start.6 = (f32[16,2,16,128]{3,2,1,0:T(8,128)S(1)}, f32[16,2,16,128]{3,2,1,0:T(8,128)S(1)}, u32[]{:S(2)}, u32[]{:S(2)}) collective-permute-start(f32[16,2,16,128]{3,2,1,0:T(8,128)S(1)} %get-tuple-element.30), channel_id=1, source_target_pairs={{0,2},{2,4},{4,6},{6,0},{8,10},{10,12},{12,14},{14,8},{1,3},{3,5},... | collective-permute-start | bytes 786440 | tf_op jit(solution)/shard_map/ppermute | solution.py:540
  57.5 7.4 %collective-permute-start.7 = (f32[16,2,16,128]{3,2,1,0:T(8,128)S(1)}, f32[16,2,16,128]{3,2,1,0:T(8,128)S(1)}, u32[]{:S(2)}, u32[]{:S(2)}) collective-permute-start(f32[16,2,16,128]{3,2,1,0:T(8,128)S(1)} %get-tuple-element.29), channel_id=1, source_target_pairs={{0,16},{16,32},{32,48},{48,64},{64,80},{80,96},{96,112},{112,0},{1... | collective-permute-start | bytes 786440 | tf_op jit(solution)/shard_map/ppermute | solution.py:541
  69.0 5.2 %collective-permute-start.8 = (f32[16,2,32,128]{3,2,1,0:T(8,128)S(1)}, f32[16,2,32,128]{3,2,1,0:T(8,128)S(1)}, u32[]{:S(2)}, u32[]{:S(2)}) collective-permute-start(f32[16,2,32,128]{3,2,1,0:T(8,128)S(1)} %get-tuple-element.28), channel_id=1, source_target_pairs={{0,1},{1,0},{2,3},{3,2},{4,5},{5,4},{6,7},{7,6},{8,9},{9,8},{10,11... | collective-permute-start | bytes 1572872 | tf_op jit(solution)/shard_map/ppermute | solution.py:510

commit v4 on v3

--- a/solution.py
+++ b/solution.py
@@ -204,7 +204,7 @@
     )(grid)
 
 
-RING_X, RING_Y, RING_Z = 4, 4, 8
+RING_X, RING_Z = 4, 8
 
 
 def forward_rec_kernel(grid_ref, out_ref, rows_ref, sems):
@@ -355,13 +355,12 @@
         out_specs=VMEM,
         scratch_shapes=[pltpu.VMEM((768, 256), BF16)],
         out_shape=jax.ShapeDtypeStruct((slots, STEPS, channels, 128, 128), F32),
-        cost_estimate=pl.CostEstimate(flops=6 * 10**9, bytes_accessed=7 * 10**6, transcendentals=0),
         compiler_params=pltpu.CompilerParams(vmem_limit_bytes=40 * 1024 * 1024),
     )(turns, mine, other, lane, row)
 
 
 def product_kernel(
-    factor, own_ref, up_a, up_b, far_a, far_b, down_a, down_b, lig_ref, lane_ref, row_ref,
+    factor, own_ref, up_a, up_b, far_ref, down_a, down_b, lig_ref, lane_ref, row_ref,
     mine_ref, other_ref, lane_work, back_work, planes,
 ):
     place = lax.axis_index("slab")
@@ -374,14 +373,13 @@
     back_row = row_stack(signed(row_ref[...], 64, 64, -1.0, -1.0, 1.0))
     own = pl.ds(pl.multiple_of(place * 32, 32), 32)
     far = pl.ds(pl.multiple_of(32 - place * 32, 32), 32)
-    rest = [(up_a, up_b), (far_a, far_b), (down_a, down_b)]
+    held = [own_ref, (up_a, up_b), far_ref, (down_a, down_b)]
 
     def tile(turn, piece):
-        if turn == 0:
-            ref, at = own_ref, 2 * piece
-        else:
-            half = own_ref.shape[0] // 4
-            ref, at = rest[turn - 1][piece // half], 2 * (piece % half)
+        ref, at = held[turn], 2 * piece
+        if isinstance(ref, tuple):
+            half = ref[0].shape[0]
+            ref, at = ref[at // half], at % half
         return jnp.concatenate([ref[at + p, s ^ place] for s in range(2) for p in range(2)], axis=0)
 
     left = lax.broadcasted_iota(jnp.int32, (slots * 64, 128), 1) < 64
@@ -495,11 +493,6 @@
     return [(yh * RING_X + x, yh * RING_X + (x + step) % RING_X) for yh in range(2) for x in range(RING_X)]
 
 
-def shift_y(step):
-    place = lambda y, x: (y % 2) * 2 * RING_X + (y // 2) * RING_X + x
-    return [(place(y, x), place((y + step) % RING_Y, x)) for y in range(RING_Y) for x in range(RING_X)]
-
-
 def shift_z(step):
     return [(z, (z + step) % RING_Z) for z in range(RING_Z)]
 
@@ -535,8 +528,7 @@
         block,
         lax.ppermute(first, "lig", shift_x(-1)),
         lax.ppermute(second, "z", shift_z(-1)),
-        lax.ppermute(first, ("yl", "lig"), shift_y(1)),
-        lax.ppermute(second, ("yl", "lig"), shift_y(-1)),
+        lax.ppermute(block, "yl", [(0, 1), (1, 0)]),
         lax.ppermute(first, "lig", shift_x(1)),
         lax.ppermute(second, "z", shift_z(1)),
     ]

time: 75.9 us -> 74 us (0.975)
  starting transfers between devices: 23.1 us -> 18.9 us
  waiting for transfers between devices: 9.64 us -> 11.7 us
    ppermute x2 -> x1, starting transfers between devices: 2.58 us -> 0.01 us  [per_device(): lax.ppermute(block, 'yl', [(0, 1), (1, 0)])]
    ppermute x2 -> x1, waiting for transfers between devices: 0.01 us -> 1.93 us  [per_device(): lax.ppermute(block, 'yl', [(0, 1), (1, 0)])]
    ppermute x1, starting transfers between devices: 1.51 us -> 0.33 us  [per_device(): lax.ppermute(second, 'z', shift_z(1))]
  transfers between devices with their start and end apart: 10 -> 9, of which waited for: 2 -> 4; matrix products, arithmetic and copies ran while one was open for 0% -> 0% of each run, Pallas kernels for 9% -> 10%
where the time goes in v4:
time: 74 us; the launch traced here: 73.7 us
  blocking collectives  27.1 us (37%)
  starting transfers between devices  18.9 us (26%)
  Pallas kernels  15.1 us (20%)
  waiting for transfers between devices  11.7 us (16%)
  between operations  0.77 us (1%)
    all_to_all x1, blocking collectives, per_device(): lax.all_to_all(jnp.broadcast_to(piece, (len(groups[0]), *piece.shape[1:])...  27.1 us
    all_to_all x1, starting transfers between devices, per_device(): lax.all_to_all(rec_share, ('yl', 'z'), split_axis=0, concat_axis=0)  10.1 us
    all_to_all x1, waiting for transfers between devices, per_device(): lax.all_to_all(rec_share, ('yl', 'z'), split_axis=0, concat_axis=0)  8.08 us
    pallas_call x1, Pallas kernels, spectrum(): pl.pallas_call(spectrum_kernel, in_specs=[SMEM, VMEM, VMEM, VMEM, VMEM],...  5.88 us
    ppermute x3, starting transfers between devices, per_device(): swap = lambda value: lax.ppermute(value, 'slab', [(0, 1), (1, 0)])  5.76 us
    pallas_call x1, Pallas kernels, product(): pl.pallas_call(lambda *refs: product_kernel(factor, *refs), in_specs=[VME...  4.24 us
    pallas_call x1, Pallas kernels, forward_rec(): pl.pallas_call(forward_rec_kernel, in_specs=[pl.BlockSpec(memory_space=pl...  2.41 us
    ppermute x1, waiting for transfers between devices, per_device(): lax.ppermute(block, 'yl', [(0, 1), (1, 0)])  1.93 us
  transfers between devices with their start and end apart: 9, of which 4 were waited for; matrix products, arithmetic and copies ran while one was open for 0% of the time, Pallas kernels for 10%

profile of v4, /device:TPU:1, one launch (start us, length us, event | category | flops | bytes accessed | tf_op | source)
XLA Modules:
  0.0 73.7 jit_solution(11182823621090741447)
XLA Ops:
  0.0 2.4 %shard_map.64 = f32[16,2,16,128]{3,2,1,0:T(8,128)} custom-call(f32[128,4096]{1,0:T(8,128)} %bitcast.15), custom_call_target="tpu_custom_call" | custom-call | tf_op jit(solution)/shard_map/pallas_call | solution.py:241
  2.4 10.1 %all-to-all-start = ((f32[16,2,16,128]{3,2,1,0:T(8,128)}), f32[16,2,16,128]{3,2,1,0:T(8,128)S(1)}, u32[]{:S(2)}, u32[]{:S(2)}) async-start(f32[16,2,16,128]{3,2,1,0:T(8,128)} %shard_map.64), calls=%async_computation | async-start | bytes 524288 | tf_op jit(solution)/shard_map/all_to_all | solution.py:508
  13.2 8.1 %all-to-all-done = f32[16,2,16,128]{3,2,1,0:T(8,128)S(1)} async-done(((f32[16,2,16,128]{3,2,1,0:T(8,128)}), f32[16,2,16,128]{3,2,1,0:T(8,128)S(1)}, u32[]{:S(2)}, u32[]{:S(2)}) %all-to-all-start) | async-done | bytes 262176 | tf_op jit(solution)/shard_map/all_to_all | solution.py:508
  21.3 2.3 %collective-permute-start = (f32[16,128]{1,0:T(8,128)S(1)}, f32[16,128]{1,0:T(8,128)S(1)}, u32[]{:S(2)}, u32[]{:S(2)}) collective-permute-start(f32[16,128]{1,0:T(8,128)S(1)} %get-tuple-element.32), channel_id=1, source_target_pairs={{0,1},{1,0},{2,3},{3,2},{4,5},{5,4},{6,7},{7,6},{8,9},{9,8},{10,11... | collective-permute-start | bytes 24584 | tf_op jit(solution)/shard_map/ppermute | solution.py:503
  23.6 1.1 %shard_map.65 = (f32[16,128,128]{2,1,0:T(8,128)S(1)}, f32[16,128,128]{2,1,0:T(8,128)S(1)}) custom-call(f32[128,4096]{1,0:T(8,128)S(1)} %bitcast.14), custom_call_target="tpu_custom_call" | custom-call | flops 3000000000 | bytes 4000000 | tf_op jit(solution)/shard_map/pallas_call | solution.py:197
  24.8 0.0 copy-start
  24.8 0.0 copy-start.1
  24.8 0.0 copy-start.2
  24.9 0.1 collective-permute-start.1
  25.0 0.1 broadcast_in_dim.4
  25.0 27.1 %all_to_all.10.refs_0_ = f32[32,2,16,128]{3,2,1,0:T(8,128)S(1)} all-to-all(f32[32,2,16,128]{3,2,1,0:T(8,128)S(1)} %broadcast_in_dim.4), channel_id=1, replica_groups={{0,8,22,30,36,44,50,58,64,72,86,94,100,108,114,122,132,140,146,154,160,..., dimensions={0} | all-to-all | bytes 1048576 | tf_op jit(solution)/shard_map/all_to_all | solution.py:518
  52.1 0.0 collective-permute-done.1.other_ref
  52.1 0.0 collective-permute-start.4
  52.2 0.9 %collective-permute-start.2 = (f32[16,2,16,128]{3,2,1,0:T(8,128)S(1)}, f32[16,2,16,128]{3,2,1,0:T(8,128)S(1)}, u32[]{:S(2)}, u32[]{:S(2)}) collective-permute-start(f32[16,2,16,128]{3,2,1,0:T(8,128)S(1)} %get-tuple-element.30), channel_id=1, source_target_pairs={{0,6},{2,0},{4,2},{6,4},{8,14},{10,8},{12,10},{14,12},{1,7},{3,1},... | collective-permute-start | bytes 786440 | tf_op jit(solution)/shard_map/ppermute | solution.py:529
  53.1 0.9 %collective-permute-start.3 = (f32[16,2,16,128]{3,2,1,0:T(8,128)S(1)}, f32[16,2,16,128]{3,2,1,0:T(8,128)S(1)}, u32[]{:S(2)}, u32[]{:S(2)}) collective-permute-start(f32[16,2,16,128]{3,2,1,0:T(8,128)S(1)} %get-tuple-element.29), channel_id=1, source_target_pairs={{0,112},{16,0},{32,16},{48,32},{64,48},{80,64},{96,80},{112,96},{1... | collective-permute-start | bytes 786440 | tf_op jit(solution)/shard_map/ppermute | solution.py:530
  54.0 0.8 %collective-permute-start.5 = (f32[16,2,16,128]{3,2,1,0:T(8,128)S(1)}, f32[16,2,16,128]{3,2,1,0:T(8,128)S(1)}, u32[]{:S(2)}, u32[]{:S(2)}) collective-permute-start(f32[16,2,16,128]{3,2,1,0:T(8,128)S(1)} %get-tuple-element.30), channel_id=1, source_target_pairs={{0,2},{2,4},{4,6},{6,0},{8,10},{10,12},{12,14},{14,8},{1,3},{3,5},... | collective-permute-start | bytes 786440 | tf_op jit(solution)/shard_map/ppermute | solution.py:532
  54.8 0.3 collective-permute-start.6
  55.2 5.9 %shard_map.66.refs_6_ = f32[2,9,4,128,128]{4,3,2,1,0:T(8,128)S(1)} custom-call(s32[2]{0:T(128)S(1)} %copy-done.2, f32[16,128,128]{2,1,0:T(8,128)S(1)} %get-tuple-element.25.mine_ref, f32[16,128,128]{2,1,0:T(8,128)S(1)} %collective-permute-done.1.other_ref, f32[2,256,256]{2,1,0:T(8,128)S(1)} %copy-done, f32[128,128]{1,0:T(8,128)S(1)} %copy-done.1), custom_call_target="tpu_custom_call" | custom-call | tf_op jit(solution)/shard_map/pallas_call | solution.py:352
  61.1 0.2 collective-permute-done.6.refs_5_
  61.3 1.9 %collective-permute-done.4.refs_3_ = f32[32,2,16,128]{3,2,1,0:T(8,128)S(1)} collective-permute-done((f32[32,2,16,128]{3,2,1,0:T(8,128)S(1)}, f32[32,2,16,128]{3,2,1,0:T(8,128)S(1)}, u32[]{:S(2)}, u32[]{:S(2)}) %collective-permute-start.4) | collective-permute-done | bytes 524320 | tf_op jit(solution)/shard_map/ppermute | solution.py:531
  63.2 4.2 %shard_map.67 = (f32[16,2,32,128]{3,2,1,0:T(8,128)S(1)}, f32[16,2,32,128]{3,2,1,0:T(8,128)S(1)}) custom-call(f32[32,2,16,128]{3,2,1,0:T(8,128)S(1)} %all_to_all.10.refs_0_, f32[16,2,16,128]{3,2,1,0:T(8,128)S(1)} %collective-permute-done.2.refs_1_, f32[16,2,16,128]{3,2,1,0:T(8,128)S(1)} %collective-permute-done.3.refs_2_, ...), custom_call_target="tpu_custom_call" | custom-call | tf_op jit(solution)/shard_map/pallas_call | solution.py:429
  67.4 3.3 %collective-permute-start.7 = (f32[16,2,32,128]{3,2,1,0:T(8,128)S(1)}, f32[16,2,32,128]{3,2,1,0:T(8,128)S(1)}, u32[]{:S(2)}, u32[]{:S(2)}) collective-permute-start(f32[16,2,32,128]{3,2,1,0:T(8,128)S(1)} %get-tuple-element.28), channel_id=1, source_target_pairs={{0,1},{1,0},{2,3},{3,2},{4,5},{5,4},{6,7},{7,6},{8,9},{9,8},{10,11... | collective-permute-start | bytes 1572872 | tf_op jit(solution)/shard_map/ppermute | solution.py:503
  70.7 1.5 %collective-permute-done.7.other_ref = f32[16,2,32,128]{3,2,1,0:T(8,128)S(1)} collective-permute-done((f32[16,2,32,128]{3,2,1,0:T(8,128)S(1)}, f32[16,2,32,128]{3,2,1,0:T(8,128)S(1)}, u32[]{:S(2)}, u32[]{:S(2)}) %collective-permute-start.7) | collective-permute-done | bytes 524320 | tf_op jit(solution)/shard_map/ppermute | solution.py:503
  72.3 1.4 %shard_map.68 = f32[2,32,4096]{2,1,0:T(8,128)} custom-call(f32[16,2,32,128]{3,2,1,0:T(8,128)S(1)} %get-tuple-element.27.mine_ref, f32[16,2,32,128]{3,2,1,0:T(8,128)S(1)} %collective-permute-done.7.other_ref), custom_call_target="tpu_custom_call" | custom-call | tf_op jit(solution)/shard_map/pallas_call | solution.py:465
  (12 shorter events, 0.1 us)
Async XLA Ops:
  0.0 23.6 %copy-start.3 = (f32[1,4,32,4096]{3,2,1,0:T(8,128)S(1)}, f32[1,4,32,4096]{3,2,1,0:T(8,128)}, u32[]{:S(2)}) copy-start(f32[1,4,32,4096]{3,2,1,0:T(8,128)} %param.7) | copy-start | bytes 6291460
  2.4 18.9 %all-to-all-start = ((f32[16,2,16,128]{3,2,1,0:T(8,128)}), f32[16,2,16,128]{3,2,1,0:T(8,128)S(1)}, u32[]{:S(2)}, u32[]{:S(2)}) async-start(f32[16,2,16,128]{3,2,1,0:T(8,128)} %shard_map.64), calls=%async_computation | async-start | bytes 524288 | tf_op jit(solution)/shard_map/all_to_all | solution.py:508
  21.3 3.5 %collective-permute-start = (f32[16,128]{1,0:T(8,128)S(1)}, f32[16,128]{1,0:T(8,128)S(1)}, u32[]{:S(2)}, u32[]{:S(2)}) collective-permute-start(f32[16,128]{1,0:T(8,128)S(1)} %get-tuple-element.32), channel_id=1, source_target_pairs={{0,1},{1,0},{2,3},{3,2},{4,5},{5,4},{6,7},{7,6},{8,9},{9,8},{10,11... | collective-permute-start | bytes 24584 | tf_op jit(solution)/shard_map/ppermute | solution.py:503
  24.8 30.4 %copy-start = (f32[2,256,256]{2,1,0:T(8,128)S(1)}, f32[2,256,256]{2,1,0:T(8,128)}, u32[]{:S(2)}) copy-start(f32[2,256,256]{2,1,0:T(8,128)} %constant.10.clone.lane_ref.refs_7_) | copy-start | bytes 1572868
  24.8 30.4 %copy-start.1 = (f32[128,128]{1,0:T(8,128)S(1)}, f32[128,128]{1,0:T(8,128)}, u32[]{:S(2)}) copy-start(f32[128,128]{1,0:T(8,128)} %constant.11.clone.row_ref.refs_8_) | copy-start | bytes 196612
  24.8 30.4 %copy-start.2 = (s32[2]{0:T(128)S(1)}, s32[2]{0:T(128)}, u32[]{:S(2)}) copy-start(s32[2]{0:T(128)} %turn_ref.1) | copy-start | bytes 28
  24.9 27.3 %collective-permute-start.1 = (f32[16,128,128]{2,1,0:T(8,128)S(1)}, f32[16,128,128]{2,1,0:T(8,128)S(1)}, u32[]{:S(2)}, u32[]{:S(2)}) collective-permute-start(f32[16,128,128]{2,1,0:T(8,128)S(1)} %get-tuple-element.23), channel_id=1, source_target_pairs={{0,1},{1,0},{2,3},{3,2},{4,5},{5,4},{6,7},{7,6},{8,9},{9,8},{10,11... | collective-permute-start | bytes 3145736 | tf_op jit(solution)/shard_map/ppermute | solution.py:503
  52.1 11.1 %collective-permute-start.4 = (f32[32,2,16,128]{3,2,1,0:T(8,128)S(1)}, f32[32,2,16,128]{3,2,1,0:T(8,128)S(1)}, u32[]{:S(2)}, u32[]{:S(2)}) collective-permute-start(f32[32,2,16,128]{3,2,1,0:T(8,128)S(1)} %all_to_all.10.refs_0_), channel_id=1, source_target_pairs={{0,128},{128,0},{1,129},{129,1},{2,130},{130,2},{3,131},{131,3},{4... | collective-permute-start | bytes 1572872 | tf_op jit(solution)/shard_map/ppermute | solution.py:531
  52.2 8.9 %collective-permute-start.2 = (f32[16,2,16,128]{3,2,1,0:T(8,128)S(1)}, f32[16,2,16,128]{3,2,1,0:T(8,128)S(1)}, u32[]{:S(2)}, u32[]{:S(2)}) collective-permute-start(f32[16,2,16,128]{3,2,1,0:T(8,128)S(1)} %get-tuple-element.30), channel_id=1, source_target_pairs={{0,6},{2,0},{4,2},{6,4},{8,14},{10,8},{12,10},{14,12},{1,7},{3,1},... | collective-permute-start | bytes 786440 | tf_op jit(solution)/shard_map/ppermute | solution.py:529
  53.1 8.0 %collective-permute-start.3 = (f32[16,2,16,128]{3,2,1,0:T(8,128)S(1)}, f32[16,2,16,128]{3,2,1,0:T(8,128)S(1)}, u32[]{:S(2)}, u32[]{:S(2)}) collective-permute-start(f32[16,2,16,128]{3,2,1,0:T(8,128)S(1)} %get-tuple-element.29), channel_id=1, source_target_pairs={{0,112},{16,0},{32,16},{48,32},{64,48},{80,64},{96,80},{112,96},{1... | collective-permute-start | bytes 786440 | tf_op jit(solution)/shard_map/ppermute | solution.py:530
  54.0 7.1 %collective-permute-start.5 = (f32[16,2,16,128]{3,2,1,0:T(8,128)S(1)}, f32[16,2,16,128]{3,2,1,0:T(8,128)S(1)}, u32[]{:S(2)}, u32[]{:S(2)}) collective-permute-start(f32[16,2,16,128]{3,2,1,0:T(8,128)S(1)} %get-tuple-element.30), channel_id=1, source_target_pairs={{0,2},{2,4},{4,6},{6,0},{8,10},{10,12},{12,14},{14,8},{1,3},{3,5},... | collective-permute-start | bytes 786440 | tf_op jit(solution)/shard_map/ppermute | solution.py:532
  54.8 6.4 %collective-permute-start.6 = (f32[16,2,16,128]{3,2,1,0:T(8,128)S(1)}, f32[16,2,16,128]{3,2,1,0:T(8,128)S(1)}, u32[]{:S(2)}, u32[]{:S(2)}) collective-permute-start(f32[16,2,16,128]{3,2,1,0:T(8,128)S(1)} %get-tuple-element.29), channel_id=1, source_target_pairs={{0,16},{16,32},{32,48},{48,64},{64,80},{80,96},{96,112},{112,0},{1... | collective-permute-start | bytes 786440 | tf_op jit(solution)/shard_map/ppermute | solution.py:533
  67.4 4.8 %collective-permute-start.7 = (f32[16,2,32,128]{3,2,1,0:T(8,128)S(1)}, f32[16,2,32,128]{3,2,1,0:T(8,128)S(1)}, u32[]{:S(2)}, u32[]{:S(2)}) collective-permute-start(f32[16,2,32,128]{3,2,1,0:T(8,128)S(1)} %get-tuple-element.28), channel_id=1, source_target_pairs={{0,1},{1,0},{2,3},{3,2},{4,5},{5,4},{6,7},{7,6},{8,9},{9,8},{10,11... | collective-permute-start | bytes 1572872 | tf_op jit(solution)/shard_map/ppermute | solution.py:503
